TPU v7x, 32 devices: a whole 2x2x4 slice. The times are simulated.
32 devices in a mesh: grp: 2 (over x), slab: 16 (over z, y, core).
Axes of the slice: x: 2, y: 2, z: 4, core: 2. Of those that a mesh axis runs over, the one named last changes fastest.
Arguments:
- courant: float32 [64, 64, 256], P(('grp', 'slab')), parts along dimension 0, may hold values from 0.08 to 0.28
- wave_level: float32 [64, 64, 256], P(('grp', 'slab')), parts along dimension 0, may hold values from -6 to 6
- wave_above: float32 [64, 64, 256], P(('grp', 'slab')), parts along dimension 0, may hold values from -6 to 6
- adjoint_level: float32 [64, 64, 256], P(('grp', 'slab')), parts along dimension 0, may hold values from -6 to 6
- adjoint_above: float32 [64, 64, 256], P(('grp', 'slab')), parts along dimension 0, may hold values from -6 to 6
- residual_data: float32 [8, 2048], P(None, 'grp'), parts along dimension 1, may hold values from -6 to 6
- wavelet: float32 [512], P('grp'), parts along dimension 0, may hold values from -6 to 6
- checkpoint_step: int32 [2], P('grp'), parts along dimension 0, may hold values from 0 to 248
- source_cells: int32 [3, 512], P(None, 'grp'), parts along dimension 1, may hold values from 0 to 255, as said below
- receiver_cells: int32 [3, 2048], P(None, 'grp'), parts along dimension 1, may hold values from 0 to 255, as said below
- conv_weight: bfloat16 [54, 32], replicated, may hold values from -0.875 to 0.875
- conv_bias: float32 [32], replicated, may hold values from -4 to 4
- mix_weight: bfloat16 [32, 32], replicated, may hold values from -1 to 1
- mix_bias: float32 [32], replicated, may hold values from -4 to 4
- out_weight: bfloat16 [32], replicated, may hold values from -1 to 1
- update_cotangent: bfloat16 [64, 64, 256], P(('grp', 'slab')), parts along dimension 0, may hold values from -6 to 6
Outputs:
- gradient_image: float32 [64, 64, 256], P(('grp', 'slab')), parts along dimension 0
- adjoint_first: float32 [64, 64, 256], P(('grp', 'slab')), parts along dimension 0
- adjoint_second: float32 [64, 64, 256], P(('grp', 'slab')), parts along dimension 0
- input_gradient: float32 [64, 64, 256], P(('grp', 'slab')), parts along dimension 0
- grad_conv: float32 [108, 32], P('grp'), parts along dimension 0
- grad_conv_bias: float32 [64], P('grp'), parts along dimension 0
- grad_mix: float32 [64, 32], P('grp'), parts along dimension 0
- grad_mix_bias: float32 [64], P('grp'), parts along dimension 0
- grad_out: float32 [64], P('grp'), parts along dimension 0
There are 2 independent parts, one for each index of `grp`. A program takes and returns all parts, laid end to end along the dimension named above; an argument that names none is the same for every part. Nothing has to cross between parts.
Inputs may be any that keep to these rules, and one draw needn't show every extreme that they name: `source_cells`: row 0 is a cell index along the first grid dimension (below 32), row 1 along the second (below 64), row 2 along the third (below 256); elements may share a cell. `receiver_cells`: row 0 is a cell index along the first grid dimension (below 32), row 1 along the second (below 64), row 2 along the third (below 256); receivers may share a cell.
All inputs are finite; a program needn't handle non-finite values.
Results may differ from a plain program's by a relative error of at most 0.009.
The roundings to bfloat16 on the way count: a program that leaves them out, or rounds other values in their place, can miss the bound.
Values may be sent and summed in bfloat16 or wider, within the bound.
A program may use at most 128 MiB of HBM per device.

v0:
```python
import jax
import jax.numpy as jnp
from jax import lax
from jax.sharding import PartitionSpec as P

NSTEP = 8


def with_halo(block, sides, width):
    for axis, dim in sides:
        count = lax.axis_size(axis)
        forward = [(i, i + 1) for i in range(count - 1)]
        backward = [(target, source) for source, target in forward]
        low = lax.ppermute(
            lax.slice_in_dim(block, block.shape[dim] - width, None, axis=dim), axis, forward
        )
        high = lax.ppermute(lax.slice_in_dim(block, 0, width, axis=dim), axis, backward)
        block = jnp.concatenate([low, block, high], axis=dim)
    return block


def laplace_inner(volume):
    middle = volume[1:-1]
    padded = jnp.pad(middle, ((0, 0), (1, 1), (1, 1)))
    return (
        volume[2:]
        + volume[:-2]
        + padded[:, 2:, 1:-1]
        + padded[:, :-2, 1:-1]
        + padded[:, 1:-1, 2:]
        + padded[:, 1:-1, :-2]
        - 6.0 * middle
    )


def silu_slope(values):
    sigmoid_part = jax.nn.sigmoid(values)
    return sigmoid_part * (1.0 + values * (1.0 - sigmoid_part))


def make_patches(window):
    planes = window.shape[1] - 2
    rows_all = window.shape[2] - 2
    cols_all = window.shape[3] - 2
    pieces = []
    for channel in range(2):
        for shift_z in range(3):
            for shift_x in range(3):
                for shift_y in range(3):
                    pieces.append(
                        window[
                            channel,
                            shift_z : shift_z + planes,
                            shift_x : shift_x + rows_all,
                            shift_y : shift_y + cols_all,
                        ]
                    )
    return jnp.stack(pieces)


def spread_taps(tap_fields):
    padded = jnp.pad(tap_fields, ((0, 0), (0, 0), (1, 1), (1, 1)))
    rows_all = tap_fields.shape[2]
    cols_all = tap_fields.shape[3]
    spreads = []
    for shift_z in range(3):
        running = jnp.zeros(tap_fields.shape[1:], jnp.float32)
        for shift_x in range(3):
            for shift_y in range(3):
                tap_index = 9 * shift_z + 3 * shift_x + shift_y
                running = (
                    running
                    + padded[
                        tap_index,
                        :,
                        2 - shift_x : 2 - shift_x + rows_all,
                        2 - shift_y : 2 - shift_y + cols_all,
                    ]
                )
        spreads.append(running)
    return jnp.stack(spreads)


def plane_index_of(cell_list, first_plane, thickness):
    inside = (cell_list[0] >= first_plane) & (cell_list[0] < first_plane + thickness)
    return jnp.where(inside, cell_list[0] - first_plane, thickness)


def build_forcing(source_cells, receiver_cells, residual_data, lead_plane, shape_lead):
    thickness = shape_lead[0]
    source_plane = plane_index_of(source_cells, lead_plane, thickness)
    source_count = (
        jnp.zeros(shape_lead, jnp.float32)
        .at[source_plane, source_cells[1], source_cells[2]]
        .add(jnp.ones((source_cells.shape[1],), jnp.float32), mode="drop")
    )
    record_plane = plane_index_of(receiver_cells, lead_plane, thickness)
    record_fields = (
        jnp.zeros((residual_data.shape[0],) + tuple(shape_lead), jnp.float32)
        .at[:, record_plane, receiver_cells[1], receiver_cells[2]]
        .add(residual_data, mode="drop")
    )
    return (source_count, record_fields)


def forcing(level_now, offset, thickness, extras):
    wavelet, checkpoint_step, source_count, record_fields = extras
    pulse_value = lax.dynamic_slice_in_dim(wavelet, checkpoint_step[0] + level_now - 1, 1)
    sources = source_count[offset : offset + thickness] * pulse_value[0]
    step_fields = lax.dynamic_index_in_dim(record_fields, level_now - 1, 0, keepdims=False)
    records = step_fields[offset : offset + thickness]
    return (sources, records)


def advance(
    lap_wave,
    lap_adjoint,
    wave_now,
    wave_upper,
    adjoint_now,
    adjoint_upper,
    coefficient,
    sources,
    records,
):
    lower_wave = 2.0 * wave_now - wave_upper + coefficient * lap_wave + sources
    lower_adjoint = 2.0 * adjoint_now - adjoint_upper + lap_adjoint + records
    return (lower_wave, lower_adjoint)


def on_device(
    courant,
    wave_level,
    wave_above,
    adjoint_level,
    adjoint_above,
    residual_data,
    wavelet,
    checkpoint_step,
    source_cells,
    receiver_cells,
    conv_weight,
    conv_bias,
    mix_weight,
    mix_bias,
    out_weight,
    update_cotangent,
):
    planes = courant.shape[0]
    own_shape = courant.shape
    base_plane = lax.axis_index("slab") * planes
    grid_planes = lax.axis_size("slab") * planes
    shape_lead = (planes + 4,) + tuple(own_shape[1:])
    source_count, record_fields = build_forcing(
        source_cells, receiver_cells, residual_data, base_plane - 2, shape_lead
    )
    extras = (wavelet, checkpoint_step, source_count, record_fields)
    start_state = (wave_level, wave_above, adjoint_level, adjoint_above, jnp.zeros_like(courant))

    def one_turn(turn_index, carried):
        current, upper_wave, adjoint, upper_adjoint, image_sum = carried
        level_now = NSTEP - turn_index
        sent_pair = jnp.stack([current, courant * adjoint])
        widened = with_halo(sent_pair, (("slab", 1),), 1)
        lap_wave = laplace_inner(widened[0])
        lap_adjoint = laplace_inner(widened[1])
        image_sum = image_sum + adjoint * lap_wave
        sources, records = forcing(level_now, 2, planes, extras)
        lower_wave, lower_adjoint = advance(
            lap_wave,
            lap_adjoint,
            current,
            upper_wave,
            adjoint,
            upper_adjoint,
            courant,
            sources,
            records,
        )
        return (lower_wave, current, lower_adjoint, adjoint, image_sum)

    final_state = lax.fori_loop(0, NSTEP, one_turn, start_state)
    image_sum = final_state[4]
    floats = jnp.float32
    cnn_input = jnp.stack([image_sum, courant]).astype(jnp.bfloat16)
    input_wide = with_halo(cnn_input, (("slab", 1),), 1)
    window = jnp.pad(input_wide, ((0, 0), (0, 0), (1, 1), (1, 1)))
    patches = make_patches(window)
    pre_one = (
        jnp.einsum("kc,kzxy->czxy", conv_weight, patches, preferred_element_type=floats)
        + conv_bias[:, None, None, None]
    )
    act_one = jax.nn.silu(pre_one).astype(jnp.bfloat16)
    pre_two = (
        jnp.einsum("dc,dzxy->czxy", mix_weight, act_one, preferred_element_type=floats)
        + mix_bias[:, None, None, None]
    )
    act_two = jax.nn.silu(pre_two).astype(jnp.bfloat16)
    cot_two = out_weight.astype(floats)[:, None, None, None] * update_cotangent.astype(floats)[None]
    grad_pre_two = (cot_two * silu_slope(pre_two)).astype(jnp.bfloat16)
    grad_out = jnp.einsum("czxy,zxy->c", act_two, update_cotangent, preferred_element_type=floats)
    grad_mix_bias = jnp.sum(grad_pre_two, axis=(1, 2, 3), dtype=floats)
    grad_mix = jnp.einsum("dzxy,czxy->dc", act_one, grad_pre_two, preferred_element_type=floats)
    cot_one = jnp.einsum("dc,czxy->dzxy", mix_weight, grad_pre_two, preferred_element_type=floats)
    grad_pre_one = (cot_one * silu_slope(pre_one)).astype(jnp.bfloat16)
    grad_conv_bias = jnp.sum(grad_pre_one, axis=(1, 2, 3), dtype=floats)
    grad_conv = jnp.einsum("kzxy,czxy->kc", patches, grad_pre_one, preferred_element_type=floats)
    image_weight = conv_weight[: conv_weight.shape[0] // 2]
    cotangent_wide = with_halo(grad_pre_one, (("slab", 1),), 1)
    tap_fields = jnp.einsum(
        "tc,czxy->tzxy", image_weight, cotangent_wide, preferred_element_type=floats
    )
    spreads = spread_taps(tap_fields)
    input_gradient = spreads[1, 1:-1] + spreads[2, :-2] + spreads[0, 2:]
    summed = lax.psum((grad_conv, grad_conv_bias, grad_mix, grad_mix_bias, grad_out), "slab")
    grad_scale = float(grid_planes * own_shape[1] * own_shape[2]) ** (-0.5)
    return (
        image_sum,
        final_state[2],
        final_state[3],
        input_gradient,
        summed[0] * grad_scale,
        summed[1] * grad_scale,
        summed[2] * grad_scale,
        summed[3] * grad_scale,
        summed[4] * grad_scale,
    )


def solution(mesh):
    return jax.shard_map(
        on_device,
        mesh=mesh,
        in_specs=(
            P(("grp", "slab"), None, None),
            P(("grp", "slab"), None, None),
            P(("grp", "slab"), None, None),
            P(("grp", "slab"), None, None),
            P(("grp", "slab"), None, None),
            P(None, "grp"),
            P("grp"),
            P("grp"),
            P(None, "grp"),
            P(None, "grp"),
            P(),
            P(),
            P(),
            P(),
            P(),
            P(("grp", "slab"), None, None),
        ),
        out_specs=(
            P(("grp", "slab"), None, None),
            P(("grp", "slab"), None, None),
            P(("grp", "slab"), None, None),
            P(("grp", "slab"), None, None),
            P("grp", None),
            P("grp"),
            P("grp", None),
            P("grp"),
            P("grp"),
        ),
        check_vma=False,
    )
```

profile of v0, /device:TPU:0, one launch (start us, length us, event | category | flops | bytes accessed | tf_op | source)
XLA Modules:
  0.0 320.8 jit_solution(1458789963754395882)
XLA Ops:
  4.0 25.8 %scatter_custom_fusion.1 = f32[8,98304]{0,1:T(8,128)} fusion(s32[1024]{0:T(1024)S(1)} %broadcast_select_fusion, f32[1024,8]{1,0:T(8,128)S(1)} %copy.33, f32[]{:T(128)} %constant.136.clone.1), kind=kCustom, calls=%fused_computation.61 | custom fusion | flops 8192 | bytes 3145732
  29.8 29.7 %copy.34 = f32[8,6,64,256]{3,2,1,0:T(8,128)} copy(f32[8,6,64,256]{0,3,2,1:T(8,128)} %bitcast.145) | data formatting | bytes 6291456
  59.6 16.2 %scatter_fusion = f32[6,64,256]{2,1,0:T(8,128)S(1)} fusion(f32[6,64,256]{2,1,0:T(8,128)S(1)} %broadcast_in_dim.35, s32[256]{0:T(256)S(1)} %bitcast.152, f32[256]{0:T(256)S(1)} %broadcast.245), kind=kCustom, calls=%fused_computation | custom fusion | flops 256 | bytes 6144 | tf_op jit(solution)/shard_map/scatter-add | solution.py:95
  75.9 87.2 %while.27 = (s32[]{:T(128)}, f32[2,64,256]{2,1,0:T(8,128)S(1)}, f32[2,64,256]{2,1,0:T(8,128)S(1)}, f32[2,64,256]{2,1,0:T(8,128)S(1)}, f32[2,64,256]{2,1,0:T(8,12...) while((s32[]{:T(128)}, f32[2,64,256]{2,1,0:T(8,128)S(1)}, ...), condition=%wide.region_3.4_spmd.clone, body=%wide.region_2.3_spmd.clone.sunk | while | flops 1245198 | bytes 6160799 | solution.py:182
  76.0 2.3 collective-permute-start
  78.3 1.3 collective-permute-start.1
  80.8 2.8 collective-permute-done.1
  83.8 1.7 fusion.103
  85.7 5.5 %collective-permute-start = (f32[2,1,64,256]{3,2,1,0:T(8,128)S(1)}, f32[2,1,64,256]{3,2,1,0:T(8,128)S(1)}, u32[]{:S(2)}, u32[]{:S(2)}) collective-permute-start(f32[2,1,64,256]{3,2,1,0:T(8,128)S(1)} %get-tuple-element.645), channel_id=1, source_target_pairs={{0,1},{1,2},{2,3},{3,4},{4,5},{5,6},{6,7},{7,8},{8,9},{9,10},{10,1... | collective-permute-start | bytes 393224 | tf_op jit(solution)/shard_map/while/body/eval_jaxpr/ppermute | solution.py:14
  91.1 1.3 collective-permute-start.1
  94.5 1.7 fusion.103
  96.4 5.8 %collective-permute-start = (f32[2,1,64,256]{3,2,1,0:T(8,128)S(1)}, f32[2,1,64,256]{3,2,1,0:T(8,128)S(1)}, u32[]{:S(2)}, u32[]{:S(2)}) collective-permute-start(f32[2,1,64,256]{3,2,1,0:T(8,128)S(1)} %get-tuple-element.645), channel_id=1, source_target_pairs={{0,1},{1,2},{2,3},{3,4},{4,5},{5,6},{6,7},{7,8},{8,9},{9,10},{10,1... | collective-permute-start | bytes 393224 | tf_op jit(solution)/shard_map/while/body/eval_jaxpr/ppermute | solution.py:14
  102.2 1.3 collective-permute-start.1
  105.6 1.7 fusion.103
  107.4 5.9 %collective-permute-start = (f32[2,1,64,256]{3,2,1,0:T(8,128)S(1)}, f32[2,1,64,256]{3,2,1,0:T(8,128)S(1)}, u32[]{:S(2)}, u32[]{:S(2)}) collective-permute-start(f32[2,1,64,256]{3,2,1,0:T(8,128)S(1)} %get-tuple-element.645), channel_id=1, source_target_pairs={{0,1},{1,2},{2,3},{3,4},{4,5},{5,6},{6,7},{7,8},{8,9},{9,10},{10,1... | collective-permute-start | bytes 393224 | tf_op jit(solution)/shard_map/while/body/eval_jaxpr/ppermute | solution.py:14
  113.3 1.3 collective-permute-start.1
  116.7 1.7 fusion.103
  118.6 5.9 %collective-permute-start = (f32[2,1,64,256]{3,2,1,0:T(8,128)S(1)}, f32[2,1,64,256]{3,2,1,0:T(8,128)S(1)}, u32[]{:S(2)}, u32[]{:S(2)}) collective-permute-start(f32[2,1,64,256]{3,2,1,0:T(8,128)S(1)} %get-tuple-element.645), channel_id=1, source_target_pairs={{0,1},{1,2},{2,3},{3,4},{4,5},{5,6},{6,7},{7,8},{8,9},{9,10},{10,1... | collective-permute-start | bytes 393224 | tf_op jit(solution)/shard_map/while/body/eval_jaxpr/ppermute | solution.py:14
  124.5 1.3 collective-permute-start.1
  127.9 1.7 fusion.103
  129.7 5.9 %collective-permute-start = (f32[2,1,64,256]{3,2,1,0:T(8,128)S(1)}, f32[2,1,64,256]{3,2,1,0:T(8,128)S(1)}, u32[]{:S(2)}, u32[]{:S(2)}) collective-permute-start(f32[2,1,64,256]{3,2,1,0:T(8,128)S(1)} %get-tuple-element.645), channel_id=1, source_target_pairs={{0,1},{1,2},{2,3},{3,4},{4,5},{5,6},{6,7},{7,8},{8,9},{9,10},{10,1... | collective-permute-start | bytes 393224 | tf_op jit(solution)/shard_map/while/body/eval_jaxpr/ppermute | solution.py:14
  135.6 1.3 collective-permute-start.1
  139.0 1.7 fusion.103
  140.9 5.9 %collective-permute-start = (f32[2,1,64,256]{3,2,1,0:T(8,128)S(1)}, f32[2,1,64,256]{3,2,1,0:T(8,128)S(1)}, u32[]{:S(2)}, u32[]{:S(2)}) collective-permute-start(f32[2,1,64,256]{3,2,1,0:T(8,128)S(1)} %get-tuple-element.645), channel_id=1, source_target_pairs={{0,1},{1,2},{2,3},{3,4},{4,5},{5,6},{6,7},{7,8},{8,9},{9,10},{10,1... | collective-permute-start | bytes 393224 | tf_op jit(solution)/shard_map/while/body/eval_jaxpr/ppermute | solution.py:14
  146.7 1.3 collective-permute-start.1
  150.1 1.7 fusion.103
  152.0 5.9 %collective-permute-start = (f32[2,1,64,256]{3,2,1,0:T(8,128)S(1)}, f32[2,1,64,256]{3,2,1,0:T(8,128)S(1)}, u32[]{:S(2)}, u32[]{:S(2)}) collective-permute-start(f32[2,1,64,256]{3,2,1,0:T(8,128)S(1)} %get-tuple-element.645), channel_id=1, source_target_pairs={{0,1},{1,2},{2,3},{3,4},{4,5},{5,6},{6,7},{7,8},{8,9},{9,10},{10,1... | collective-permute-start | bytes 393224 | tf_op jit(solution)/shard_map/while/body/eval_jaxpr/ppermute | solution.py:14
  157.9 1.3 collective-permute-start.1
  161.3 1.7 fusion.103
  163.7 5.9 %collective-permute-start.2 = (bf16[2,1,64,256]{3,0,2,1:T(2,128)(2,1)S(1)}, bf16[2,1,64,256]{3,0,2,1:T(2,128)(2,1)S(1)}, u32[]{:S(2)}, u32[]{:S(2)}) collective-permute-start(bf16[2,1,64,256]{3,0,2,1:T(2,128)(2,1)S(1)} %get-tuple-element.557), channel_id=1, source_target_pairs={{0,1},{1,2},{2,3},{3,4},{4,5},{5,6},{6,7},{7,8},{8,9},{9,10},{10,1... | collective-permute-start | bytes 196616 | tf_op jit(solution)/shard_map/ppermute | solution.py:14
  169.5 1.5 collective-permute-start.3
  172.7 2.3 select_maximum_fusion
  175.0 3.5 %fusion.92 = (bf16[1,2,64,256]{3,0,2,1:T(2,128)(2,1)S(1)}, bf16[1,2,64,256]{3,0,2,1:T(2,128)(2,1)S(1)}, bf16[1,2,64,256]{3,0,2,1:T(2,128)(2,1)S(1)}, bf16[1,2,64...) fusion(bf16[2,4,66,258]{3,0,2,1:T(2,128)(2,1)S(1)} %select_maxi, ...), kind=kLoop, calls=%fused_computation.183 | loop fusion | bytes 2490368 | tf_op jit(solution)/shard_map/slice | solution.py:51
  178.5 3.8 %fusion.93 = (bf16[1,2,64,256]{3,0,2,1:T(2,128)(2,1)S(1)}, bf16[1,2,64,256]{3,0,2,1:T(2,128)(2,1)S(1)}, bf16[1,2,64,256]{3,0,2,1:T(2,128)(2,1)S(1)}, bf16[1,2,64...) fusion(bf16[2,4,66,258]{3,0,2,1:T(2,128)(2,1)S(1)} %select_maxi, ...), kind=kLoop, calls=%fused_computation.184 | loop fusion | bytes 2490368 | tf_op jit(solution)/shard_map/slice | solution.py:51
  182.4 2.0 fusion.94
  185.0 1.0 fusion.95
  186.0 23.1 %stack.63 = bf16[54,2,64,256]{3,0,2,1:T(8,128)(2,1)} concatenate(bf16[1,2,64,256]{3,0,2,1:T(2,128)(2,1)} %get-tuple-element.554, bf16[1,2,64,256]{3,0,2,1:T(2,128)(2,1)} %get-tuple-element.553, bf16[1,2,64,256]{3,0,2,1:T(2,128)(2,1)} %get-tuple-element.552, bf16[1,2,64,256]{3,0,2,1:T(2,128)(2,1)} %get-tuple-element.551, bf16[1,2,64,256]{3,0,2,1:T(2,128)(2,1)S(1)} %get-tuple-element.570, ...), dimensions={0} | concatenate | bytes 7077888 | tf_op jit(solution)/shard_map/stack | solution.py:58
  209.2 3.5 %fusion.36 = (bf16[32,2,64,256]{3,0,2,1:T(8,128)(2,1)S(1)}, f32[2,64,256,32]{2,3,1,0:T(8,128)S(1)}) fusion(f32[32]{0:T(128)} %param.29, bf16[54,2,64,256]{3,0,2,1:T(8,128)(2,1)} %stack.63, bf16[54,32]{0,1:T(8,128)(2,1)S(1)} %copy-done.13), kind=kOutput, calls=%fused_computation.88 | convolution fusion | flops 119537664 | bytes 9833984 | tf_op jit(solution)/shard_map/kc,kzxy->czxy/dot_general | solution.py:190
  212.7 3.1 convert_reduce_fusion
  216.5 2.2 convert_reduce_fusion.1
  218.7 1.1 fusion.55
  219.8 1.2 fusion.91
  221.0 6.2 %collective-permute-start.4 = (bf16[32,1,64,256]{3,0,2,1:T(8,128)(2,1)}, bf16[32,1,64,256]{3,0,2,1:T(8,128)(2,1)}, u32[]{:S(2)}, u32[]{:S(2)}) collective-permute-start(bf16[32,1,64,256]{3,0,2,1:T(8,128)(2,1)} %get-tuple-element.505), channel_id=1, source_target_pairs={{0,1},{1,2},{2,3},{3,4},{4,5},{5,6},{6,7},{7,8},{8,9},{9,10},{10,1... | collective-permute-start | bytes 3145736 | tf_op jit(solution)/shard_map/ppermute | solution.py:14
  227.2 1.3 collective-permute-start.5
  229.1 72.8 %all-reduce.4 = (f32[54,32]{0,1:T(8,128)S(1)}, f32[32]{0:T(128)S(1)}, f32[32,32]{1,0:T(8,128)S(1)}, f32[32]{0:T(128)S(1)}, f32[32]{0:T(128)S(1)}) all-reduce(f32[54,32]{0,1:T(8,128)S(1)} %fusion.55, f32[32]{0:T(128)S(1)} %get-tuple-element.568, f32[32,32]{1,0:T(8,128)S(1)} %fusion.50, ...), channel_id=1, replica_groups=mesh['grp'=2,'slab'=16] {'slab'}, use_global_device_ids=true, to_apply=%region_4.5 | all-reduce | flops 2848 | bytes 22784 | tf_op jit(solution)/shard_map/psum | solution.py:215
  304.7 2.7 fusion.41
  307.5 11.2 %fusion.69 = (f32[1,4,64,256]{3,0,2,1:T(1,128)S(1)}, f32[1,4,64,256]{3,0,2,1:T(1,128)S(1)}, f32[1,4,64,256]{3,0,2,1:T(1,128)S(1)}, f32[1,4,64,256]{3,0,2,1:T(1,1...) fusion(f32[27,4,64,256]{3,0,2,1:T(8,128)S(1)} %fusion.41), kind=kLoop, calls=%fused_computation.115 | loop fusion | flops 393216 | bytes 13893632 | tf_op jit(solution)/shard_map/add | solution.py:72
  319.0 1.1 fusion.74
  (149 shorter events, 22.8 us)
Async XLA Ops:
  0.6 212.0 %copy-start = (bf16[32,32]{1,0:T(8,128)(2,1)S(1)}, bf16[32,32]{1,0:T(8,128)(2,1)}, u32[]{:S(2)}) copy-start(bf16[32,32]{1,0:T(8,128)(2,1)} %param.30) | copy-start | bytes 6148
  29.8 29.7 %copy-start.14 = (s32[3,256]{1,0:T(4,128)S(1)}, s32[3,256]{1,0:T(4,128)}, u32[]{:S(2)}) copy-start(s32[3,256]{1,0:T(4,128)} %param.26) | copy-start | bytes 9220
  29.8 29.7 %copy-start.4 = (f32[2,64,256]{2,1,0:T(8,128)S(1)}, f32[2,64,256]{2,1,0:T(8,128)}, u32[]{:S(2)}) copy-start(f32[2,64,256]{2,1,0:T(8,128)} %param.18) | copy-start | bytes 393220
  29.8 46.0 %copy-start.1 = (f32[2,64,256]{2,1,0:T(8,128)S(1)}, f32[2,64,256]{2,1,0:T(8,128)}, u32[]{:S(2)}) copy-start(f32[2,64,256]{2,1,0:T(8,128)} %param.19) | copy-start | bytes 393220
  29.8 46.1 %copy-start.3 = (f32[2,64,256]{2,1,0:T(8,128)S(1)}, f32[2,64,256]{2,1,0:T(8,128)}, u32[]{:S(2)}) copy-start(f32[2,64,256]{2,1,0:T(8,128)} %param.21) | copy-start | bytes 393220
  29.8 46.1 %copy-start.5 = (f32[2,64,256]{2,1,0:T(8,128)S(1)}, f32[2,64,256]{2,1,0:T(8,128)}, u32[]{:S(2)}) copy-start(f32[2,64,256]{2,1,0:T(8,128)} %param.20) | copy-start | bytes 393220
  29.8 46.1 %copy-start.7 = (f32[2,64,256]{2,1,0:T(8,128)S(1)}, f32[2,64,256]{2,1,0:T(8,128)}, u32[]{:S(2)}) copy-start(f32[2,64,256]{2,1,0:T(8,128)} %param.22) | copy-start | bytes 393220
  29.8 46.1 %copy-start.15 = (f32[256]{0:T(256)S(1)}, f32[256]{0:T(256)}, u32[]{:S(2)}) copy-start(f32[256]{0:T(256)} %param.24) | copy-start | bytes 3076
  75.9 95.1 %copy-start.11 = (bf16[2,64,256]{2,1,0:T(8,128)(2,1)S(1)}, bf16[2,64,256]{2,1,0:T(8,128)(2,1)}, u32[]{:S(2)}) copy-start(bf16[2,64,256]{2,1,0:T(8,128)(2,1)} %param.33) | copy-start | bytes 196612
  75.9 95.8 %copy-start.16 = (bf16[32]{0:T(256)(128)(2,1)S(1)}, bf16[32]{0:T(256)(128)(2,1)}, u32[]{:S(2)}) copy-start(bf16[32]{0:T(256)(128)(2,1)} %param.32) | copy-start | bytes 196
  76.0 4.9 %collective-permute-start = (f32[2,1,64,256]{3,2,1,0:T(8,128)S(1)}, f32[2,1,64,256]{3,2,1,0:T(8,128)S(1)}, u32[]{:S(2)}, u32[]{:S(2)}) collective-permute-start(f32[2,1,64,256]{3,2,1,0:T(8,128)S(1)} %get-tuple-element.645), channel_id=1, source_target_pairs={{0,1},{1,2},{2,3},{3,4},{4,5},{5,6},{6,7},{7,8},{8,9},{9,10},{10,1... | collective-permute-start | bytes 393224 | tf_op jit(solution)/shard_map/while/body/eval_jaxpr/ppermute | solution.py:14
  78.3 5.4 %collective-permute-start.1 = (f32[2,1,64,256]{3,2,1,0:T(8,128)S(1)}, f32[2,1,64,256]{3,2,1,0:T(8,128)S(1)}, u32[]{:S(2)}, u32[]{:S(2)}) collective-permute-start(f32[2,1,64,256]{3,2,1,0:T(8,128)S(1)} %get-tuple-element.646), channel_id=1, source_target_pairs={{1,0},{2,1},{3,2},{4,3},{5,4},{6,5},{7,6},{8,7},{9,8},{10,9},{11,1... | collective-permute-start | bytes 393224 | tf_op jit(solution)/shard_map/while/body/eval_jaxpr/ppermute | solution.py:17
  85.7 8.0 %collective-permute-start = (f32[2,1,64,256]{3,2,1,0:T(8,128)S(1)}, f32[2,1,64,256]{3,2,1,0:T(8,128)S(1)}, u32[]{:S(2)}, u32[]{:S(2)}) collective-permute-start(f32[2,1,64,256]{3,2,1,0:T(8,128)S(1)} %get-tuple-element.645), channel_id=1, source_target_pairs={{0,1},{1,2},{2,3},{3,4},{4,5},{5,6},{6,7},{7,8},{8,9},{9,10},{10,1... | collective-permute-start | bytes 393224 | tf_op jit(solution)/shard_map/while/body/eval_jaxpr/ppermute | solution.py:14
  91.1 3.2 %collective-permute-start.1 = (f32[2,1,64,256]{3,2,1,0:T(8,128)S(1)}, f32[2,1,64,256]{3,2,1,0:T(8,128)S(1)}, u32[]{:S(2)}, u32[]{:S(2)}) collective-permute-start(f32[2,1,64,256]{3,2,1,0:T(8,128)S(1)} %get-tuple-element.646), channel_id=1, source_target_pairs={{1,0},{2,1},{3,2},{4,3},{5,4},{6,5},{7,6},{8,7},{9,8},{10,9},{11,1... | collective-permute-start | bytes 393224 | tf_op jit(solution)/shard_map/while/body/eval_jaxpr/ppermute | solution.py:17
  96.4 8.3 %collective-permute-start = (f32[2,1,64,256]{3,2,1,0:T(8,128)S(1)}, f32[2,1,64,256]{3,2,1,0:T(8,128)S(1)}, u32[]{:S(2)}, u32[]{:S(2)}) collective-permute-start(f32[2,1,64,256]{3,2,1,0:T(8,128)S(1)} %get-tuple-element.645), channel_id=1, source_target_pairs={{0,1},{1,2},{2,3},{3,4},{4,5},{5,6},{6,7},{7,8},{8,9},{9,10},{10,1... | collective-permute-start | bytes 393224 | tf_op jit(solution)/shard_map/while/body/eval_jaxpr/ppermute | solution.py:14
  102.2 3.2 %collective-permute-start.1 = (f32[2,1,64,256]{3,2,1,0:T(8,128)S(1)}, f32[2,1,64,256]{3,2,1,0:T(8,128)S(1)}, u32[]{:S(2)}, u32[]{:S(2)}) collective-permute-start(f32[2,1,64,256]{3,2,1,0:T(8,128)S(1)} %get-tuple-element.646), channel_id=1, source_target_pairs={{1,0},{2,1},{3,2},{4,3},{5,4},{6,5},{7,6},{8,7},{9,8},{10,9},{11,1... | collective-permute-start | bytes 393224 | tf_op jit(solution)/shard_map/while/body/eval_jaxpr/ppermute | solution.py:17
  107.4 8.4 %collective-permute-start = (f32[2,1,64,256]{3,2,1,0:T(8,128)S(1)}, f32[2,1,64,256]{3,2,1,0:T(8,128)S(1)}, u32[]{:S(2)}, u32[]{:S(2)}) collective-permute-start(f32[2,1,64,256]{3,2,1,0:T(8,128)S(1)} %get-tuple-element.645), channel_id=1, source_target_pairs={{0,1},{1,2},{2,3},{3,4},{4,5},{5,6},{6,7},{7,8},{8,9},{9,10},{10,1... | collective-permute-start | bytes 393224 | tf_op jit(solution)/shard_map/while/body/eval_jaxpr/ppermute | solution.py:14
  113.3 3.2 %collective-permute-start.1 = (f32[2,1,64,256]{3,2,1,0:T(8,128)S(1)}, f32[2,1,64,256]{3,2,1,0:T(8,128)S(1)}, u32[]{:S(2)}, u32[]{:S(2)}) collective-permute-start(f32[2,1,64,256]{3,2,1,0:T(8,128)S(1)} %get-tuple-element.646), channel_id=1, source_target_pairs={{1,0},{2,1},{3,2},{4,3},{5,4},{6,5},{7,6},{8,7},{9,8},{10,9},{11,1... | collective-permute-start | bytes 393224 | tf_op jit(solution)/shard_map/while/body/eval_jaxpr/ppermute | solution.py:17
  118.6 8.4 %collective-permute-start = (f32[2,1,64,256]{3,2,1,0:T(8,128)S(1)}, f32[2,1,64,256]{3,2,1,0:T(8,128)S(1)}, u32[]{:S(2)}, u32[]{:S(2)}) collective-permute-start(f32[2,1,64,256]{3,2,1,0:T(8,128)S(1)} %get-tuple-element.645), channel_id=1, source_target_pairs={{0,1},{1,2},{2,3},{3,4},{4,5},{5,6},{6,7},{7,8},{8,9},{9,10},{10,1... | collective-permute-start | bytes 393224 | tf_op jit(solution)/shard_map/while/body/eval_jaxpr/ppermute | solution.py:14
  124.5 3.2 %collective-permute-start.1 = (f32[2,1,64,256]{3,2,1,0:T(8,128)S(1)}, f32[2,1,64,256]{3,2,1,0:T(8,128)S(1)}, u32[]{:S(2)}, u32[]{:S(2)}) collective-permute-start(f32[2,1,64,256]{3,2,1,0:T(8,128)S(1)} %get-tuple-element.646), channel_id=1, source_target_pairs={{1,0},{2,1},{3,2},{4,3},{5,4},{6,5},{7,6},{8,7},{9,8},{10,9},{11,1... | collective-permute-start | bytes 393224 | tf_op jit(solution)/shard_map/while/body/eval_jaxpr/ppermute | solution.py:17
  129.7 8.4 %collective-permute-start = (f32[2,1,64,256]{3,2,1,0:T(8,128)S(1)}, f32[2,1,64,256]{3,2,1,0:T(8,128)S(1)}, u32[]{:S(2)}, u32[]{:S(2)}) collective-permute-start(f32[2,1,64,256]{3,2,1,0:T(8,128)S(1)} %get-tuple-element.645), channel_id=1, source_target_pairs={{0,1},{1,2},{2,3},{3,4},{4,5},{5,6},{6,7},{7,8},{8,9},{9,10},{10,1... | collective-permute-start | bytes 393224 | tf_op jit(solution)/shard_map/while/body/eval_jaxpr/ppermute | solution.py:14
  135.6 3.2 %collective-permute-start.1 = (f32[2,1,64,256]{3,2,1,0:T(8,128)S(1)}, f32[2,1,64,256]{3,2,1,0:T(8,128)S(1)}, u32[]{:S(2)}, u32[]{:S(2)}) collective-permute-start(f32[2,1,64,256]{3,2,1,0:T(8,128)S(1)} %get-tuple-element.646), channel_id=1, source_target_pairs={{1,0},{2,1},{3,2},{4,3},{5,4},{6,5},{7,6},{8,7},{9,8},{10,9},{11,1... | collective-permute-start | bytes 393224 | tf_op jit(solution)/shard_map/while/body/eval_jaxpr/ppermute | solution.py:17
  140.9 8.4 %collective-permute-start = (f32[2,1,64,256]{3,2,1,0:T(8,128)S(1)}, f32[2,1,64,256]{3,2,1,0:T(8,128)S(1)}, u32[]{:S(2)}, u32[]{:S(2)}) collective-permute-start(f32[2,1,64,256]{3,2,1,0:T(8,128)S(1)} %get-tuple-element.645), channel_id=1, source_target_pairs={{0,1},{1,2},{2,3},{3,4},{4,5},{5,6},{6,7},{7,8},{8,9},{9,10},{10,1... | collective-permute-start | bytes 393224 | tf_op jit(solution)/shard_map/while/body/eval_jaxpr/ppermute | solution.py:14
  146.7 3.2 %collective-permute-start.1 = (f32[2,1,64,256]{3,2,1,0:T(8,128)S(1)}, f32[2,1,64,256]{3,2,1,0:T(8,128)S(1)}, u32[]{:S(2)}, u32[]{:S(2)}) collective-permute-start(f32[2,1,64,256]{3,2,1,0:T(8,128)S(1)} %get-tuple-element.646), channel_id=1, source_target_pairs={{1,0},{2,1},{3,2},{4,3},{5,4},{6,5},{7,6},{8,7},{9,8},{10,9},{11,1... | collective-permute-start | bytes 393224 | tf_op jit(solution)/shard_map/while/body/eval_jaxpr/ppermute | solution.py:17
  152.0 8.4 %collective-permute-start = (f32[2,1,64,256]{3,2,1,0:T(8,128)S(1)}, f32[2,1,64,256]{3,2,1,0:T(8,128)S(1)}, u32[]{:S(2)}, u32[]{:S(2)}) collective-permute-start(f32[2,1,64,256]{3,2,1,0:T(8,128)S(1)} %get-tuple-element.645), channel_id=1, source_target_pairs={{0,1},{1,2},{2,3},{3,4},{4,5},{5,6},{6,7},{7,8},{8,9},{9,10},{10,1... | collective-permute-start | bytes 393224 | tf_op jit(solution)/shard_map/while/body/eval_jaxpr/ppermute | solution.py:14
  157.9 3.2 %collective-permute-start.1 = (f32[2,1,64,256]{3,2,1,0:T(8,128)S(1)}, f32[2,1,64,256]{3,2,1,0:T(8,128)S(1)}, u32[]{:S(2)}, u32[]{:S(2)}) collective-permute-start(f32[2,1,64,256]{3,2,1,0:T(8,128)S(1)} %get-tuple-element.646), channel_id=1, source_target_pairs={{1,0},{2,1},{3,2},{4,3},{5,4},{6,5},{7,6},{8,7},{9,8},{10,9},{11,1... | collective-permute-start | bytes 393224 | tf_op jit(solution)/shard_map/while/body/eval_jaxpr/ppermute | solution.py:17
  163.1 19.3 %copy-start.2 = (f32[2,64,256]{2,1,0:T(8,128)}, f32[2,64,256]{2,1,0:T(8,128)S(1)}, u32[]{:S(2)}) copy-start(f32[2,64,256]{2,1,0:T(8,128)S(1)} %get-tuple-element.379) | copy-start | bytes 393220
  163.1 19.3 %copy-start.6 = (f32[2,64,256]{2,1,0:T(8,128)}, f32[2,64,256]{2,1,0:T(8,128)S(1)}, u32[]{:S(2)}) copy-start(f32[2,64,256]{2,1,0:T(8,128)S(1)} %get-tuple-element.380) | copy-start | bytes 393220
  163.1 19.3 %copy-start.8 = (f32[2,64,256]{2,1,0:T(8,128)}, f32[2,64,256]{2,1,0:T(8,128)S(1)}, u32[]{:S(2)}) copy-start(f32[2,64,256]{2,1,0:T(8,128)S(1)} %get-tuple-element.378) | copy-start | bytes 393220
  163.7 8.5 %collective-permute-start.2 = (bf16[2,1,64,256]{3,0,2,1:T(2,128)(2,1)S(1)}, bf16[2,1,64,256]{3,0,2,1:T(2,128)(2,1)S(1)}, u32[]{:S(2)}, u32[]{:S(2)}) collective-permute-start(bf16[2,1,64,256]{3,0,2,1:T(2,128)(2,1)S(1)} %get-tuple-element.557), channel_id=1, source_target_pairs={{0,1},{1,2},{2,3},{3,4},{4,5},{5,6},{6,7},{7,8},{8,9},{9,10},{10,1... | collective-permute-start | bytes 196616 | tf_op jit(solution)/shard_map/ppermute | solution.py:14
  169.5 3.1 collective-permute-start.3
  186.0 23.1 %copy-start.13 = (bf16[54,32]{0,1:T(8,128)(2,1)S(1)}, bf16[54,32]{0,1:T(8,128)(2,1)}, u32[]{:S(2)}) copy-start(bf16[54,32]{0,1:T(8,128)(2,1)} %param.28) | copy-start | bytes 10372
  209.2 3.5 %copy-start.10 = (f32[2,64,256]{2,1,0:T(8,128)S(1)}, f32[2,64,256]{2,1,0:T(8,128)}, u32[]{:S(2)}) copy-start(f32[2,64,256]{2,1,0:T(8,128)} %convert_element_type.39) | copy-start | bytes 393220
  209.2 3.5 %copy-start.17 = (f32[32]{0:T(128)S(1)}, f32[32]{0:T(128)}, u32[]{:S(2)}) copy-start(f32[32]{0:T(128)} %param.31) | copy-start | bytes 388
  209.2 3.5 %copy-start.19 = (f32[32]{0:T(128)S(1)}, f32[32]{0:T(128)}, u32[]{:S(2)}) copy-start(f32[32]{0:T(128)} %convert_element_type.38) | copy-start | bytes 388
  215.8 0.7 copy-start.18
  216.4 2.2 copy-start.9
  218.6 9.9 %copy-start.12 = (bf16[2,64,256]{2,1,0:T(8,128)(2,1)S(1)}, bf16[2,64,256]{2,1,0:T(8,128)(2,1)}, u32[]{:S(2)}) copy-start(bf16[2,64,256]{2,1,0:T(8,128)(2,1)} %param.33) | copy-start | bytes 196612
  221.0 83.8 %collective-permute-start.4 = (bf16[32,1,64,256]{3,0,2,1:T(8,128)(2,1)}, bf16[32,1,64,256]{3,0,2,1:T(8,128)(2,1)}, u32[]{:S(2)}, u32[]{:S(2)}) collective-permute-start(bf16[32,1,64,256]{3,0,2,1:T(8,128)(2,1)} %get-tuple-element.505), channel_id=1, source_target_pairs={{0,1},{1,2},{2,3},{3,4},{4,5},{5,6},{6,7},{7,8},{8,9},{9,10},{10,1... | collective-permute-start | bytes 3145736 | tf_op jit(solution)/shard_map/ppermute | solution.py:14
  227.2 77.5 %collective-permute-start.5 = (bf16[32,1,64,256]{3,0,2,1:T(8,128)(2,1)S(1)}, bf16[32,1,64,256]{3,0,2,1:T(8,128)(2,1)}, u32[]{:S(2)}, u32[]{:S(2)}) collective-permute-start(bf16[32,1,64,256]{3,0,2,1:T(8,128)(2,1)S(1)} %get-tuple-element.506), channel_id=1, source_target_pairs={{1,0},{2,1},{3,2},{4,3},{5,4},{6,5},{7,6},{8,7},{9,8},{10,9},{11,1... | collective-permute-start | bytes 3145736 | tf_op jit(solution)/shard_map/ppermute | solution.py:17
where the time goes:
time: 323 us; the launch traced here: 321 us
  other arithmetic  79.1 us (24%)
  blocking collectives  72.8 us (23%)
  local copies, waits for them, and re-layouts  71.7 us (22%)
  starting transfers between devices  68 us (21%)
  matrix products  13.9 us (4%)
  waiting for transfers between devices  8.14 us (3%)
  loops' own time  6.02 us (2%)
    psum x1, blocking collectives, on_device(): lax.psum((grad_conv, grad_conv_bias, grad_mix, grad_mix_bias, grad_out),...  72.8 us
    ppermute x10, starting transfers between devices, with_halo(): lax.ppermute(lax.slice_in_dim(block, block.shape[dim] - width, None, axis...  54.9 us
    unnamed x43, local copies, waits for them, and re-layouts  31.4 us
    unnamed x5, other arithmetic  27.3 us
    another operation x1, local copies, waits for them, and re-layouts, make_patches(): return jnp.stack(pieces)  23.1 us
    scatter-add x1, other arithmetic, build_forcing(): source_count = jnp.zeros(shape_lead, jnp.float32).at[source_plane, source...  16.2 us
    add x8, other arithmetic, advance(): lower_adjoint = 2.0 * adjoint_now - adjoint_upper + lap_adjoint + records  13.7 us
    ppermute x10, starting transfers between devices, with_halo(): lax.ppermute(lax.slice_in_dim(block, 0, width, axis=dim), axis, backward)  13.1 us
  transfers between devices with their start and end apart: 20, of which 9 were waited for; matrix products, arithmetic and copies ran while one was open for 3% of the time, Pallas kernels for 0%

commit v1 on v0

v1 whole, which is shorter than its diff:
```python
import functools

import jax
import jax.numpy as jnp
import numpy as np
from jax import lax
from jax.experimental import pallas as pl
from jax.experimental.pallas import tpu as pltpu
from jax.sharding import PartitionSpec as P

NSTEP = 8
RB = 8
SR = 24
QR = 16
LANE_BIAS, LANE_MIX, LANE_MIX_BIAS, LANE_OUT = 54, 64, 96, 97
EXCH_IMAGE, EXCH_COURANT, EXCH_SPREAD, EXCH_COUNT = 16, 17, 18, 19
F32 = jnp.float32
BF16 = jnp.bfloat16


def tap_row(h, a, b, c):
    return 27 * h + 9 * a + 3 * b + c


def constants(taps, hidden):
    rep = np.zeros((RB * hidden, hidden), np.float32)
    for x in range(RB):
        rep[x * hidden : (x + 1) * hidden] = np.eye(hidden)
    wide = (RB + 2) * SR
    sel = np.zeros((3, taps, wide), np.float32)
    place = np.zeros((3, wide, 128), np.float32)
    for x in range(RB + 2):
        for b in range(3):
            for h in range(2):
                for a in range(3):
                    for c in range(3):
                        column = x * SR + h * 9 + a * 3 + c
                        sel[b, tap_row(h, a, b, c), column] = 1
                        place[b, column, tap_row(h, a, b, c)] = 1
        place[1, x * SR + 18, LANE_BIAS] = 1
    back = np.zeros((3, (RB + 2) * QR, taps), np.float32)
    for x in range(RB + 2):
        for b in range(3):
            for a in range(3):
                for c in range(3):
                    back[b, x * QR + a * 3 + c, tap_row(0, a, b, c)] = 1
    column_block = (np.arange(wide) // SR).astype(np.int32)[None]
    return (
        jnp.asarray(rep, BF16),
        jnp.asarray(sel, BF16),
        jnp.asarray(place, F32),
        jnp.asarray(back, BF16),
        jnp.asarray(column_block),
    )


def dot(a, b):
    return lax.dot_general(a, b, (((1,), (0,)), ((), ())), preferred_element_type=F32)


def dot_nt(a, b):
    return lax.dot_general(a, b, (((1,), (1,)), ((), ())), preferred_element_type=F32)


def dot_exact(a, b):
    return lax.dot_general(
        a, b, (((1,), (0,)), ((), ())), preferred_element_type=F32, precision=lax.Precision.HIGHEST
    )


def kernel(
    n,
    grad_scale,
    step_ref,
    courant,
    wave_level,
    wave_above,
    adjoint_level,
    adjoint_above,
    residual,
    wavelet,
    source_cells,
    receiver_cells,
    conv_weight,
    conv_bias,
    mix_weight,
    mix_bias,
    out_weight,
    cotangent,
    rep_ref,
    sel_ref,
    place_ref,
    back_ref,
    block_ref,
    image_out,
    first_out,
    second_out,
    input_out,
    grad_conv_out,
    grad_conv_bias_out,
    grad_mix_out,
    grad_mix_bias_out,
    grad_out_out,
    wave,
    adj,
    scaled,
    halo,
    onehot_rec,
    window,
    bf_planes,
    bf_halo,
    cot_rows,
    t_conv,
    t_mix,
    t_mix_back,
    t_taps,
    t_out,
    taps_sum,
    acc_conv,
    acc_mix,
    acc_small,
    spread_send,
    spread_halo,
    reduce_send,
    reduce_recv,
    send_sem,
    recv_sem,
    red_send_sem,
    red_recv_sem,
):
    planes, nx, ny = courant.shape
    hidden = mix_weight.shape[0]
    me = lax.axis_index("slab")
    last = n - 1
    up_id = lax.rem(me + 1, n)
    down_id = lax.rem(me + n - 1, n)
    stages = n.bit_length() - 1
    has_low = me > 0
    has_high = me < last

    barrier = pltpu.get_barrier_semaphore()

    def greet(target):
        pl.semaphore_signal(
            barrier, inc=1, device_id={"slab": target}, device_id_type=pl.DeviceIdType.MESH
        )

    @pl.when(has_low)
    def _():
        greet(down_id)

    @pl.when(has_high)
    def _():
        greet(up_id)

    def partner(stage):
        bit = 1 << stage
        return me + bit - 2 * bit * lax.rem(me // bit, 2)

    for stage in range(stages):
        greet(partner(stage))

    def remote(src, dst, ssem, rsem, target):
        return pltpu.make_async_remote_copy(
            src_ref=src,
            dst_ref=dst,
            send_sem=ssem,
            recv_sem=rsem,
            device_id={"slab": target},
            device_id_type=pl.DeviceIdType.MESH,
        )

    def pair(which, up_src, up_dst, down_src, down_dst):
        up = lambda: remote(up_src, up_dst, send_sem.at[which, 0], recv_sem.at[which, 0], up_id)
        down = lambda: remote(
            down_src, down_dst, send_sem.at[which, 1], recv_sem.at[which, 1], down_id
        )

        def start():
            @pl.when(has_high)
            def _():
                up().start()

            @pl.when(has_low)
            def _():
                down().start()

        def wait_recv():
            @pl.when(has_low)
            def _():
                up().wait_recv()

            @pl.when(has_high)
            def _():
                down().wait_recv()

        def wait_send():
            @pl.when(has_high)
            def _():
                up().wait_send()

            @pl.when(has_low)
            def _():
                down().wait_send()

        return start, wait_recv, wait_send

    def field_pair(turn, field):
        source = wave if field == 0 else scaled
        slot = turn + 1 if field == 0 else turn
        return pair(
            2 * turn + field,
            source.at[slot, planes - 1],
            halo.at[turn, field, 0],
            source.at[slot, 0],
            halo.at[turn, field, 1],
        )

    def bf_pair(channel):
        return pair(
            EXCH_IMAGE + channel,
            bf_planes.at[channel, planes - 1],
            bf_halo.at[channel, 0],
            bf_planes.at[channel, 0],
            bf_halo.at[channel, 1],
        )

    spread_pair = pair(
        EXCH_SPREAD,
        spread_send.at[0],
        spread_halo.at[0],
        spread_send.at[1],
        spread_halo.at[1],
    )

    wave[0] = wave_above[...]
    wave[1] = wave_level[...]
    adj[0] = adjoint_above[...]
    adj[1] = adjoint_level[...]
    scaled[0] = courant[...] * adjoint_level[...]
    bf_planes[1] = courant[...].astype(BF16)

    def clear(side):
        halo[:, :, side] = jnp.zeros(halo.shape[:2] + halo.shape[3:], F32)
        bf_halo[:, side] = jnp.zeros(bf_halo.shape[:1] + bf_halo.shape[2:], BF16)
        spread_halo[side] = jnp.zeros(spread_halo.shape[1:], F32)

    @pl.when(jnp.logical_not(has_low))
    def _():
        clear(0)

    @pl.when(jnp.logical_not(has_high))
    def _():
        clear(1)

    pl.semaphore_wait(
        barrier, jnp.where(has_low, 1, 0) + jnp.where(has_high, 1, 0) + stages
    )
    field_pair(0, 0)[0]()
    field_pair(0, 1)[0]()
    bf_pair(1)[0]()

    base = me * planes
    rows = planes * nx

    def row_hot(cells):
        count = cells.shape[1]
        place = (cells[0:1, :] - base) * nx + cells[1:2, :]
        return lax.broadcasted_iota(jnp.int32, (rows, count), 0) == place

    def column_hot(cells):
        count = cells.shape[1]
        hit = lax.broadcasted_iota(jnp.int32, (ny, count), 0) == cells[2:3, :]
        return jnp.where(hit, 1.0, 0.0).astype(BF16)

    onehot_rec[...] = column_hot(receiver_cells)
    source_rows = jnp.where(row_hot(source_cells), 1.0, 0.0).astype(BF16)
    source_count = dot_nt(source_rows, column_hot(source_cells))
    steps_of = wavelet.shape[1]
    pick = (
        lax.broadcasted_iota(jnp.int32, (NSTEP, steps_of), 1)
        == lax.broadcasted_iota(jnp.int32, (NSTEP, steps_of), 0) + step_ref[0]
    )
    pulses = jnp.sum(jnp.where(pick, wavelet[...], 0.0), axis=1, keepdims=True)

    row_id = lax.broadcasted_iota(jnp.int32, (nx, ny), 0)
    lane_id = lax.broadcasted_iota(jnp.int32, (nx, ny), 1)

    def from_left(v):
        return jnp.where(lane_id == 0, 0.0, pltpu.roll(v, 1, 1))

    def from_right(v):
        return jnp.where(lane_id == ny - 1, 0.0, pltpu.roll(v, ny - 1, 1))

    def lap_plane(v):
        total = jnp.where(row_id == nx - 1, 0.0, pltpu.roll(v, nx - 1, 0))
        total += jnp.where(row_id == 0, 0.0, pltpu.roll(v, 1, 0))
        return total + from_right(v) + from_left(v) - 6.0 * v

    def laplace(ref, slot, turn, field):
        volume = [ref[slot, p] for p in range(planes)]
        inner = [lap_plane(v) for v in volume]
        field_pair(turn, field)[1]()
        volume = [halo[turn, field, 0]] + volume + [halo[turn, field, 1]]
        return [inner[p] + volume[p] + volume[p + 2] for p in range(planes)]

    def records_of(level):
        data = residual[pl.ds(level - 1, 1), :]
        spread = jnp.where(row_hot(receiver_cells), data, 0.0)
        top = spread.astype(BF16)
        rest = spread - top.astype(F32)
        middle = rest.astype(BF16)
        low = (rest - middle.astype(F32)).astype(BF16)
        columns = onehot_rec[...]
        return dot_nt(top, columns) + (dot_nt(middle, columns) + dot_nt(low, columns))

    image_out[...] = jnp.zeros(image_out.shape, F32)

    def turn_of(turn):
        level = NSTEP - turn
        records = records_of(level)
        pulse = pulses[level - 1 : level, :]
        lap_wave = laplace(wave, turn + 1, turn, 0)
        for p in range(planes):
            cell_rows = slice(p * nx, (p + 1) * nx)
            image_out[p] += adj[turn + 1, p] * lap_wave[p]
            if turn + 1 < NSTEP:
                wave[turn + 2, p] = (
                    2.0 * wave[turn + 1, p]
                    - wave[turn, p]
                    + courant[p] * lap_wave[p]
                    + source_count[cell_rows] * pulse
                )
        if turn + 1 < NSTEP:
            field_pair(turn + 1, 0)[0]()
        lap_adj = laplace(scaled, turn, turn, 1)
        for p in range(planes):
            cell_rows = slice(p * nx, (p + 1) * nx)
            lower = 2.0 * adj[turn + 1, p] - adj[turn, p] + lap_adj[p] + records[cell_rows]
            if turn + 1 < NSTEP:
                adj[turn + 2, p] = lower
                scaled[turn + 1, p] = courant[p] * lower
            else:
                first_out[p] = lower
        if turn + 1 < NSTEP:
            field_pair(turn + 1, 1)[0]()

    def put_plane(channel, plane, values):
        shifted = (from_left(values), values, from_right(values))
        for z in range(planes):
            a = plane - z
            if 0 <= a < 3:
                for c in range(3):
                    at = SR + channel * 9 + a * 3 + c
                    for half in range(ny // 128):
                        part = shifted[c][:, half * 128 : (half + 1) * 128]
                        window[z, half, pl.ds(at, nx, stride=SR), :] = part

    window[...] = jnp.zeros(window.shape, F32)
    for z in range(planes):
        for half in range(ny // 128):
            window[z, half, pl.ds(SR + 18, nx, stride=SR), :] = jnp.ones((nx, 128), F32)
    for p in range(planes):
        put_plane(1, p + 1, bf_planes[1, p].astype(F32))
    cot_rows[...] = cotangent[...].astype(F32)

    wide = (RB + 2) * SR
    tall = RB * hidden
    rep = rep_ref[...]
    tiled = dot_nt(rep, conv_weight[...]).astype(BF16)
    row_block = lax.broadcasted_iota(jnp.int32, (tall, wide), 0) // hidden
    band = [row_block + b == block_ref[...] for b in range(3)]
    conv_banded = jnp.zeros((tall, wide), F32)
    for b in range(3):
        conv_banded += jnp.where(band[b], dot(tiled, sel_ref[b]), 0.0)
    t_conv[...] = conv_banded.astype(BF16)
    diagonal = (
        lax.broadcasted_iota(jnp.int32, (tall, tall), 0) // hidden
        == lax.broadcasted_iota(jnp.int32, (tall, tall), 1) // hidden
    )
    mixed = dot_nt(dot_nt(rep, mix_weight[...]).astype(BF16), rep)
    t_mix[...] = jnp.where(diagonal, mixed, 0.0).astype(BF16)
    mixed_back = dot_nt(dot(rep, mix_weight[...]).astype(BF16), rep)
    t_mix_back[...] = jnp.where(diagonal, mixed_back, 0.0).astype(BF16)
    back_rows = (RB + 2) * QR
    back_row = lax.broadcasted_iota(jnp.int32, (back_rows, tall), 0) // QR
    back_column = lax.broadcasted_iota(jnp.int32, (back_rows, tall), 1) // hidden
    taps_banded = jnp.zeros((back_rows, tall), F32)
    for b in range(3):
        part = dot_nt(dot(back_ref[b], conv_weight[...]).astype(BF16), rep)
        taps_banded += jnp.where(back_column + b == back_row, part, 0.0)
    t_taps[...] = taps_banded.astype(BF16)
    rep_wide = rep.astype(F32)

    def column_of(vector):
        return jnp.sum(rep_wide * vector[...].astype(F32), axis=1, keepdims=True)

    bias_one = column_of(conv_bias)
    bias_two = column_of(mix_bias)
    out_diagonal = (
        lax.broadcasted_iota(jnp.int32, (tall, RB), 0) // hidden
        == lax.broadcasted_iota(jnp.int32, (tall, RB), 1)
    )
    t_out[...] = jnp.where(out_diagonal, column_of(out_weight), 0.0).astype(BF16)
    taps_sum[...] = jnp.zeros(taps_sum.shape, F32)
    acc_conv[...] = jnp.zeros(acc_conv.shape, F32)
    acc_mix[...] = jnp.zeros(acc_mix.shape, F32)
    acc_small[...] = jnp.zeros(acc_small.shape, F32)

    for turn in range(NSTEP):
        turn_of(turn)

    for p in range(planes):
        bf_planes[0, p] = image_out[p].astype(BF16)
    bf_pair(0)[0]()
    second_out[...] = adj[NSTEP]
    for p in range(planes):
        put_plane(0, p + 1, bf_planes[0, p].astype(F32))
    bf_pair(1)[1]()
    put_plane(1, 0, bf_halo[1, 0].astype(F32))
    put_plane(1, planes + 1, bf_halo[1, 1].astype(F32))
    bf_pair(0)[1]()
    put_plane(0, 0, bf_halo[0, 0].astype(F32))
    put_plane(0, planes + 1, bf_halo[0, 1].astype(F32))

    blocks = nx // RB

    def block_of(z, x):
        where = pl.ds(pl.multiple_of(x * (RB * SR), 8), wide)
        halves = [window[z, half, where, :] for half in range(ny // 128)]
        piece = jnp.concatenate(halves, axis=1).astype(BF16)
        cot = cot_rows[z, pl.ds(pl.multiple_of(x * RB, RB), RB), :].astype(BF16)
        pre_one = dot(t_conv[...], piece) + bias_one
        sig_one = 0.5 * jnp.tanh(0.5 * pre_one) + 0.5
        act_one = (pre_one * sig_one).astype(BF16)
        slope_one = sig_one * (1.0 + pre_one * (1.0 - sig_one))
        pre_two = dot(t_mix[...], act_one) + bias_two
        sig_two = 0.5 * jnp.tanh(0.5 * pre_two) + 0.5
        act_two = (pre_two * sig_two).astype(BF16)
        slope_two = sig_two * (1.0 + pre_two * (1.0 - sig_two))
        grad_two = (dot(t_out[...], cot) * slope_two).astype(BF16)
        grad_one = (dot(t_mix_back[...], grad_two) * slope_one).astype(BF16)
        acc_conv[...] += dot_nt(grad_one, piece)
        acc_mix[...] += dot_nt(grad_two, act_one)
        acc_small[0] += dot_nt(act_two, cot)
        acc_small[1] += dot_nt(grad_two, jnp.ones((RB, ny), BF16))
        where = pl.ds(pl.multiple_of(x * (RB * QR), 8), back_rows)
        spread = dot(t_taps[...], grad_one)
        for half in range(ny // 128):
            taps_sum[z, half, where, :] += spread[:, half * 128 : (half + 1) * 128]

    def block_loop(index, carried):
        block_of(index // blocks, lax.rem(index, blocks))
        return carried

    lax.fori_loop(0, planes * blocks, block_loop, 0)

    def fold(values):
        total = values[0:hidden]
        for x in range(1, RB):
            total = total + values[x * hidden : (x + 1) * hidden]
        return total

    conv_sum = acc_conv[...]
    packed = jnp.zeros((hidden, 128), F32)
    for b in range(3):
        packed += dot_exact(fold(jnp.where(band[b], conv_sum, 0.0)), place_ref[b])
    mix_at = lax.broadcasted_iota(jnp.int32, (tall, 128), 1) - LANE_MIX
    mix_place = mix_at == lax.rem(lax.broadcasted_iota(jnp.int32, (tall, 128), 0), hidden)
    packed += dot_exact(
        fold(jnp.where(diagonal, acc_mix[...], 0.0)), jnp.where(mix_place, 1.0, 0.0)
    )
    out_sum = fold(
        jnp.sum(jnp.where(out_diagonal, acc_small[0], 0.0), axis=1, keepdims=True)
    )
    mix_bias_sum = fold(acc_small[1][:, 0:1])
    packed_lane = lax.broadcasted_iota(jnp.int32, (hidden, 128), 1)
    packed = jnp.where(packed_lane == LANE_OUT, out_sum, packed)
    packed = jnp.where(packed_lane == LANE_MIX_BIAS, mix_bias_sum, packed)

    def reduce_copy(stage):
        return remote(
            reduce_send.at[stage],
            reduce_recv.at[stage],
            red_send_sem.at[stage],
            red_recv_sem.at[stage],
            partner(stage),
        )

    reduce_send[0] = packed
    if stages:
        reduce_copy(0).start()

    def spread_of(z, a):
        base_row = QR + a * 3


        def take(c):
            where = pl.ds(base_row + c, nx, stride=QR)
            return jnp.concatenate(
                [taps_sum[z, half, where, :] for half in range(ny // 128)], axis=1
            )

        return from_right(take(0)) + take(1) + from_left(take(2))

    spread_send[0] = spread_of(planes - 1, 2)
    spread_send[1] = spread_of(0, 0)
    spread_pair[0]()

    def finish_stage(stage):
        reduce_copy(stage).wait_recv()
        reduce_send[stage + 1] = reduce_send[stage] + reduce_recv[stage]
        if stage + 1 < stages:
            reduce_copy(stage + 1).start()

    if stages:
        finish_stage(0)
    for p in range(planes):
        total = spread_of(p, 1)
        if p > 0:
            total = total + spread_of(p - 1, 2)
        if p + 1 < planes:
            total = total + spread_of(p + 1, 0)
        input_out[p] = total
    for stage in range(1, stages):
        finish_stage(stage)
    spread_pair[1]()
    input_out[0] += spread_halo[0]
    input_out[planes - 1] += spread_halo[1]

    summed = reduce_send[stages] * grad_scale
    eye = (
        lax.broadcasted_iota(jnp.int32, (128, 128), 0)
        == lax.broadcasted_iota(jnp.int32, (128, 128), 1)
    )
    turned = lax.dot_general(
        jnp.where(eye, 1.0, 0.0),
        summed,
        (((1,), (1,)), ((), ())),
        preferred_element_type=F32,
        precision=lax.Precision.HIGHEST,
    )
    taps = conv_weight.shape[0]
    grad_conv_out[...] = turned[0:taps]
    grad_conv_bias_out[...] = turned[LANE_BIAS : LANE_BIAS + 1]
    grad_mix_out[...] = turned[LANE_MIX : LANE_MIX + hidden]
    grad_mix_bias_out[...] = turned[LANE_MIX_BIAS : LANE_MIX_BIAS + 1]
    grad_out_out[...] = turned[LANE_OUT : LANE_OUT + 1]

    for turn in range(NSTEP):
        for field in range(2):
            field_pair(turn, field)[2]()
    for channel in range(2):
        bf_pair(channel)[2]()
    spread_pair[2]()
    for stage in range(stages):
        reduce_copy(stage).wait_send()


def on_device(
    courant,
    wave_level,
    wave_above,
    adjoint_level,
    adjoint_above,
    residual_data,
    wavelet,
    checkpoint_step,
    source_cells,
    receiver_cells,
    conv_weight,
    conv_bias,
    mix_weight,
    mix_bias,
    out_weight,
    update_cotangent,
):
    n = lax.axis_size("slab")
    planes, nx, ny = courant.shape
    taps, hidden = conv_weight.shape
    receivers = receiver_cells.shape[1]
    stages = n.bit_length() - 1
    grad_scale = float(n * planes * nx * ny) ** (-0.5)
    grid = (planes, nx, ny)
    tall = RB * hidden
    wide = (RB + 2) * SR
    vmem = pl.BlockSpec(memory_space=pltpu.VMEM)
    smem = pl.BlockSpec(memory_space=pltpu.SMEM)
    consts = constants(taps, hidden)
    outs = pl.pallas_call(
        functools.partial(kernel, n, grad_scale),
        out_shape=(
            jax.ShapeDtypeStruct(grid, F32),
            jax.ShapeDtypeStruct(grid, F32),
            jax.ShapeDtypeStruct(grid, F32),
            jax.ShapeDtypeStruct(grid, F32),
            jax.ShapeDtypeStruct((taps, hidden), F32),
            jax.ShapeDtypeStruct((1, hidden), F32),
            jax.ShapeDtypeStruct((hidden, hidden), F32),
            jax.ShapeDtypeStruct((1, hidden), F32),
            jax.ShapeDtypeStruct((1, hidden), F32),
        ),
        in_specs=[smem] + [vmem] * (15 + len(consts)),
        out_specs=(vmem,) * 9,
        scratch_shapes=[
            pltpu.VMEM((NSTEP + 1,) + grid, F32),
            pltpu.VMEM((NSTEP + 1,) + grid, F32),
            pltpu.VMEM((NSTEP,) + grid, F32),
            pltpu.VMEM((NSTEP, 2, 2, nx, ny), F32),
            pltpu.VMEM((ny, receivers), BF16),
            pltpu.VMEM((planes, ny // 128, (nx + 2) * SR, 128), F32),
            pltpu.VMEM((2,) + grid, BF16),
            pltpu.VMEM((2, 2, nx, ny), BF16),
            pltpu.VMEM(grid, F32),
            pltpu.VMEM((tall, wide), BF16),
            pltpu.VMEM((tall, tall), BF16),
            pltpu.VMEM((tall, tall), BF16),
            pltpu.VMEM(((RB + 2) * QR, tall), BF16),
            pltpu.VMEM((tall, RB), BF16),
            pltpu.VMEM((planes, ny // 128, (nx + 2) * QR, 128), F32),
            pltpu.VMEM((tall, wide), F32),
            pltpu.VMEM((tall, tall), F32),
            pltpu.VMEM((2, tall, RB), F32),
            pltpu.VMEM((2, nx, ny), F32),
            pltpu.VMEM((2, nx, ny), F32),
            pltpu.VMEM((stages + 1, hidden, 128), F32),
            pltpu.VMEM((max(stages, 1), hidden, 128), F32),
            pltpu.SemaphoreType.DMA((EXCH_COUNT, 2)),
            pltpu.SemaphoreType.DMA((EXCH_COUNT, 2)),
            pltpu.SemaphoreType.DMA((max(stages, 1),)),
            pltpu.SemaphoreType.DMA((max(stages, 1),)),
        ],
        compiler_params=pltpu.CompilerParams(
            collective_id=0, has_side_effects=True, vmem_limit_bytes=48 * 1024 * 1024
        ),
    )(
        checkpoint_step,
        courant,
        wave_level,
        wave_above,
        adjoint_level,
        adjoint_above,
        residual_data,
        wavelet[None],
        source_cells,
        receiver_cells,
        conv_weight,
        conv_bias[None],
        mix_weight,
        mix_bias[None],
        out_weight[None],
        update_cotangent,
        *consts,
    )
    return outs[:5] + (outs[5][0], outs[6], outs[7][0], outs[8][0])


def solution(mesh):
    slabs = P(("grp", "slab"), None, None)
    return jax.shard_map(
        on_device,
        mesh=mesh,
        in_specs=(slabs,) * 5
        + (P(None, "grp"), P("grp"), P("grp"), P(None, "grp"), P(None, "grp"))
        + (P(),) * 5
        + (slabs,),
        out_specs=(slabs,) * 4 + (P("grp", None), P("grp"), P("grp", None), P("grp"), P("grp")),
        check_vma=False,
    )
```

time: 323 us -> 80.4 us (0.25)
  other arithmetic: 79.1 us -> 0 us
  blocking collectives: 72.8 us -> 0 us
  starting transfers between devices: 68 us -> 0 us
  Pallas kernels: 0 us -> 61.5 us
  local copies, waits for them, and re-layouts: 71.7 us -> 16.7 us
  matrix products: 13.9 us -> 0 us
  waiting for transfers between devices: 8.14 us -> 0 us
  loops' own time: 6.02 us -> 0 us
    psum x1 -> x0, blocking collectives: 72.8 us -> none  [on_device(): lax.psum((grad_conv, grad_conv_bias, grad_mix, grad_mix_bias, grad_out),...]
    ppermute x20 -> x0, starting transfers between devices: 68 us -> none  [the longest x10 54.9 us: with_halo(): lax.ppermute(lax.slice_in_dim(block, block.shape[dim] - width, None, axis...]
    pallas_call x0 -> x1, Pallas kernels: none -> 61.5 us  [on_device(): pl.pallas_call(functools.partial(kernel, n, grad_scale), out_shape=(jax.S...]
    unnamed x5 -> x0, other arithmetic: 27.3 us -> none
    add x18 -> x0, other arithmetic: 27.2 us -> none  [the longest x8 13.7 us: advance(): lower_adjoint = 2.0 * adjoint_now - adjoint_upper + lap_adjoint + records]
    another operation x3 -> x0, local copies, waits for them, and re-layouts: 23.3 us -> none  [the longest x1 23.1 us: make_patches(): return jnp.stack(pieces)]
    scatter-add x1 -> x0, other arithmetic: 16.2 us -> none  [build_forcing(): source_count = jnp.zeros(shape_lead, jnp.float32).at[source_plane, source...]
    unnamed x43 -> x48, local copies, waits for them, and re-layouts: 31.4 us -> 16.7 us
  transfers between devices with their start and end apart: 20 -> 0, of which waited for: 9 -> 0; matrix products, arithmetic and copies ran while one was open for 3% -> 0% of each run, Pallas kernels for 0% -> 0%
where the time goes in v1:
time: 80.4 us; the launch traced here: 79.6 us
  Pallas kernels  61.5 us (76%)
  local copies, waits for them, and re-layouts  16.7 us (21%)
  between operations  1.44 us (2%)
    pallas_call x1, Pallas kernels, on_device(): pl.pallas_call(functools.partial(kernel, n, grad_scale), out_shape=(jax.S...  61.5 us
    unnamed x48, local copies, waits for them, and re-layouts  16.7 us

profile of v1, /device:TPU:0, one launch (start us, length us, event | category | flops | bytes accessed | tf_op | source)
XLA Modules:
  0.0 79.6 jit_solution(7257385286090819895)
XLA Ops:
  0.6 0.0 copy-start.11
  1.3 0.0 copy-start.12
  1.3 0.0 copy-start.13
  1.3 0.0 copy-start.14
  1.3 0.0 copy-start.15
  1.4 0.0 copy-start.16
  1.4 0.0 copy-start.17
  1.4 0.8 %copy.30.conv_weight = bf16[54,32]{1,0:T(8,128)(2,1)S(1)} copy(bf16[54,32]{0,1:T(8,128)(2,1)} %param.31) | data formatting | bytes 6912 | tf_op args[10]
  2.2 0.0 copy-done.11
  2.2 0.0 copy-done.12
  2.2 0.0 copy-done.13
  2.2 0.0 copy-done.14
  2.2 0.0 copy-done.15
  2.2 0.0 copy-done.16
  2.3 0.0 copy-done.17
  2.3 0.0 copy-start
  2.3 1.0 %copy-done = f32[3,240,128]{2,1,0:T(8,128)S(1)} copy-done((f32[3,240,128]{2,1,0:T(8,128)S(1)}, f32[3,240,128]{2,1,0:T(8,128)}, u32[]{:S(2)}) %copy-start) | copy-done | bytes 368664
  3.3 0.0 copy-start.1
  3.3 0.9 %copy-done.1 = f32[2,64,256]{2,1,0:T(8,128)S(1)} copy-done((f32[2,64,256]{2,1,0:T(8,128)S(1)}, f32[2,64,256]{2,1,0:T(8,128)}, u32[]{:S(2)}) %copy-start.1) | copy-done | bytes 131096
  4.2 0.0 copy-start.2
  4.2 0.9 %copy-done.2 = f32[2,64,256]{2,1,0:T(8,128)S(1)} copy-done((f32[2,64,256]{2,1,0:T(8,128)S(1)}, f32[2,64,256]{2,1,0:T(8,128)}, u32[]{:S(2)}) %copy-start.2) | copy-done | bytes 131096
  5.1 0.0 copy-start.3
  5.1 0.9 %copy-done.3 = f32[2,64,256]{2,1,0:T(8,128)S(1)} copy-done((f32[2,64,256]{2,1,0:T(8,128)S(1)}, f32[2,64,256]{2,1,0:T(8,128)}, u32[]{:S(2)}) %copy-start.3) | copy-done | bytes 131096
  6.0 0.9 %copy-done.4 = f32[2,64,256]{2,1,0:T(8,128)S(1)} copy-done((f32[2,64,256]{2,1,0:T(8,128)S(1)}, f32[2,64,256]{2,1,0:T(8,128)}, u32[]{:S(2)}) %copy-start.4) | copy-done | bytes 131096
  6.9 0.0 copy-start.5
  6.9 0.9 %copy-done.5 = f32[2,64,256]{2,1,0:T(8,128)S(1)} copy-done((f32[2,64,256]{2,1,0:T(8,128)S(1)}, f32[2,64,256]{2,1,0:T(8,128)}, u32[]{:S(2)}) %copy-start.5) | copy-done | bytes 131096
  7.8 0.0 copy-start.6
  7.8 0.9 %copy-done.6 = bf16[3,160,54]{2,1,0:T(8,128)(2,1)S(1)} copy-done((bf16[3,160,54]{2,1,0:T(8,128)(2,1)S(1)}, bf16[3,160,54]{2,1,0:T(8,128)(2,1)}, u32[]{:S(2)}) %copy-start.6) | copy-done | bytes 51864
  8.7 0.0 copy-start.7
  8.7 0.9 %copy-done.7 = bf16[3,54,240]{2,1,0:T(8,128)(2,1)S(1)} copy-done((bf16[3,54,240]{2,1,0:T(8,128)(2,1)S(1)}, bf16[3,54,240]{2,1,0:T(8,128)(2,1)}, u32[]{:S(2)}) %copy-start.7) | copy-done | bytes 77784
  9.6 0.0 copy-start.8
  9.6 0.8 %copy-done.8 = bf16[2,64,256]{2,1,0:T(8,128)(2,1)S(1)} copy-done((bf16[2,64,256]{2,1,0:T(8,128)(2,1)S(1)}, bf16[2,64,256]{2,1,0:T(8,128)(2,1)}, u32[]{:S(2)}) %copy-start.8) | copy-done | bytes 65560
  10.4 0.0 copy-start.9
  10.4 0.8 %copy-done.9 = bf16[256,32]{1,0:T(8,128)(2,1)S(1)} copy-done((bf16[256,32]{1,0:T(8,128)(2,1)S(1)}, bf16[256,32]{1,0:T(8,128)(2,1)}, u32[]{:S(2)}) %copy-start.9) | copy-done | bytes 16408
  11.3 0.0 copy-start.10
  11.3 0.8 copy-done.10
  12.0 0.0 copy-start.18
  12.0 0.7 copy-done.18
  12.7 61.5 %shard_map.268 = (f32[2,64,256]{2,1,0:T(8,128)S(1)}, f32[2,64,256]{2,1,0:T(8,128)S(1)}, f32[2,64,256]{2,1,0:T(8,128)S(1)}, f32[2,64,256]{2,1,0:T(8,128)S(1)}, f3...) custom-call(s32[1]{0:T(128)S(6)} %copy.40.step_ref, ...), custom_call_target="tpu_custom_call" | custom-call | tf_op jit(solution)/shard_map/pallas_call | solution.py:590
  74.1 0.7 copy.31
  74.8 0.7 copy.41
  75.5 0.7 copy.42
  76.1 0.7 copy.43
  76.8 0.7 copy.44
  77.4 0.5 copy.45
  78.0 0.6 copy.46
  78.6 0.5 copy.47
  79.1 0.5 copy.48
  (1 shorter events, 0.0 us)
Async XLA Ops:
  0.6 1.6 %copy-start.11 = (s32[3,1024]{1,0:T(4,128)S(1)}, s32[3,1024]{1,0:T(4,128)}, u32[]{:S(2)}) copy-start(s32[3,1024]{1,0:T(4,128)} %receiver_cells.1) | copy-start | bytes 36868
  1.3 0.9 %copy-start.12 = (bf16[32,32]{1,0:T(8,128)(2,1)S(1)}, bf16[32,32]{1,0:T(8,128)(2,1)}, u32[]{:S(2)}) copy-start(bf16[32,32]{1,0:T(8,128)(2,1)} %mix_weight.1) | copy-start | bytes 6148
  1.3 0.9 %copy-start.13 = (s32[3,256]{1,0:T(4,128)S(1)}, s32[3,256]{1,0:T(4,128)}, u32[]{:S(2)}) copy-start(s32[3,256]{1,0:T(4,128)} %source_cells.1) | copy-start | bytes 9220
  1.3 0.9 %copy-start.14 = (f32[256]{0:T(256)S(1)}, f32[256]{0:T(256)}, u32[]{:S(2)}) copy-start(f32[256]{0:T(256)} %param.27) | copy-start | bytes 3076
  1.3 0.9 %copy-start.15 = (s32[1,240]{1,0:T(1,128)S(1)}, s32[1,240]{1,0:T(1,128)}, u32[]{:S(2)}) copy-start(s32[1,240]{1,0:T(1,128)} %constant.14.clone.block_ref) | copy-start | bytes 2884
  1.4 0.9 %copy-start.16 = (f32[32]{0:T(128)S(1)}, f32[32]{0:T(128)}, u32[]{:S(2)}) copy-start(f32[32]{0:T(128)} %param.32) | copy-start | bytes 388
  1.4 0.9 %copy-start.17 = (f32[32]{0:T(128)S(1)}, f32[32]{0:T(128)}, u32[]{:S(2)}) copy-start(f32[32]{0:T(128)} %param.34) | copy-start | bytes 388
  2.3 1.0 %copy-start = (f32[3,240,128]{2,1,0:T(8,128)S(1)}, f32[3,240,128]{2,1,0:T(8,128)}, u32[]{:S(2)}) copy-start(f32[3,240,128]{2,1,0:T(8,128)} %constant.12.clone.place_ref) | copy-start | bytes 1105924
  3.3 0.9 %copy-start.1 = (f32[2,64,256]{2,1,0:T(8,128)S(1)}, f32[2,64,256]{2,1,0:T(8,128)}, u32[]{:S(2)}) copy-start(f32[2,64,256]{2,1,0:T(8,128)} %courant.1) | copy-start | bytes 393220
  4.2 0.9 %copy-start.2 = (f32[2,64,256]{2,1,0:T(8,128)S(1)}, f32[2,64,256]{2,1,0:T(8,128)}, u32[]{:S(2)}) copy-start(f32[2,64,256]{2,1,0:T(8,128)} %wave_level.1) | copy-start | bytes 393220
  5.1 0.9 %copy-start.3 = (f32[2,64,256]{2,1,0:T(8,128)S(1)}, f32[2,64,256]{2,1,0:T(8,128)}, u32[]{:S(2)}) copy-start(f32[2,64,256]{2,1,0:T(8,128)} %wave_above.1) | copy-start | bytes 393220
  6.0 0.9 %copy-start.4 = (f32[2,64,256]{2,1,0:T(8,128)S(1)}, f32[2,64,256]{2,1,0:T(8,128)}, u32[]{:S(2)}) copy-start(f32[2,64,256]{2,1,0:T(8,128)} %adjoint_level.1) | copy-start | bytes 393220
  6.9 0.9 %copy-start.5 = (f32[2,64,256]{2,1,0:T(8,128)S(1)}, f32[2,64,256]{2,1,0:T(8,128)}, u32[]{:S(2)}) copy-start(f32[2,64,256]{2,1,0:T(8,128)} %adjoint_above.1) | copy-start | bytes 393220
  7.8 0.9 %copy-start.6 = (bf16[3,160,54]{2,1,0:T(8,128)(2,1)S(1)}, bf16[3,160,54]{2,1,0:T(8,128)(2,1)}, u32[]{:S(2)}) copy-start(bf16[3,160,54]{2,1,0:T(8,128)(2,1)} %constant.13.clone.back_ref) | copy-start | bytes 155524
  8.7 0.9 %copy-start.7 = (bf16[3,54,240]{2,1,0:T(8,128)(2,1)S(1)}, bf16[3,54,240]{2,1,0:T(8,128)(2,1)}, u32[]{:S(2)}) copy-start(bf16[3,54,240]{2,1,0:T(8,128)(2,1)} %constant.11.clone.sel_ref) | copy-start | bytes 233284
  9.6 0.8 %copy-start.8 = (bf16[2,64,256]{2,1,0:T(8,128)(2,1)S(1)}, bf16[2,64,256]{2,1,0:T(8,128)(2,1)}, u32[]{:S(2)}) copy-start(bf16[2,64,256]{2,1,0:T(8,128)(2,1)} %cotangent.1) | copy-start | bytes 196612
  10.4 0.8 %copy-start.9 = (bf16[256,32]{1,0:T(8,128)(2,1)S(1)}, bf16[256,32]{1,0:T(8,128)(2,1)}, u32[]{:S(2)}) copy-start(bf16[256,32]{1,0:T(8,128)(2,1)} %constant.10.clone.rep_ref) | copy-start | bytes 49156
  11.3 0.8 copy-start.10
  12.0 0.7 copy-start.18

commit v2 on v1

--- a/solution.py
+++ b/solution.py
@@ -9,6 +9,7 @@
 from jax.sharding import PartitionSpec as P
 
 NSTEP = 8
+VMEM_LIMIT = int(63.5 * 1024 * 1024)
 RB = 8
 SR = 24
 QR = 16
@@ -71,36 +72,36 @@
 def kernel(
     n,
     grad_scale,
-    step_ref,
-    courant,
-    wave_level,
-    wave_above,
-    adjoint_level,
-    adjoint_above,
-    residual,
-    wavelet,
-    source_cells,
-    receiver_cells,
-    conv_weight,
-    conv_bias,
-    mix_weight,
-    mix_bias,
-    out_weight,
-    cotangent,
-    rep_ref,
-    sel_ref,
-    place_ref,
-    back_ref,
-    block_ref,
-    image_out,
-    first_out,
-    second_out,
-    input_out,
-    grad_conv_out,
-    grad_conv_bias_out,
-    grad_mix_out,
-    grad_mix_bias_out,
-    grad_out_out,
+    step_hbm,
+    courant_hbm,
+    wave_level_hbm,
+    wave_above_hbm,
+    adjoint_level_hbm,
+    adjoint_above_hbm,
+    residual_hbm,
+    wavelet_hbm,
+    source_cells_hbm,
+    receiver_cells_hbm,
+    conv_weight_hbm,
+    conv_bias_hbm,
+    mix_weight_hbm,
+    mix_bias_hbm,
+    out_weight_hbm,
+    cotangent_hbm,
+    rep_ref_hbm,
+    sel_ref_hbm,
+    place_ref_hbm,
+    back_ref_hbm,
+    block_ref_hbm,
+    image_out_hbm,
+    first_out_hbm,
+    second_out_hbm,
+    input_out_hbm,
+    grad_conv_out_hbm,
+    grad_conv_bias_out_hbm,
+    grad_mix_out_hbm,
+    grad_mix_bias_out_hbm,
+    grad_out_out_hbm,
     wave,
     adj,
     scaled,
@@ -127,6 +128,33 @@
     recv_sem,
     red_send_sem,
     red_recv_sem,
+    in_sem,
+    out_sem,
+    image_out,
+    first_out,
+    input_out,
+    grad_conv_out,
+    grad_conv_bias_out,
+    grad_mix_out,
+    grad_mix_bias_out,
+    grad_out_out,
+    step_ref,
+    courant,
+    residual,
+    wavelet,
+    source_cells,
+    receiver_cells,
+    conv_weight,
+    conv_bias,
+    mix_weight,
+    mix_bias,
+    out_weight,
+    cotangent,
+    rep_ref,
+    sel_ref,
+    place_ref,
+    back_ref,
+    block_ref,
 ):
     planes, nx, ny = courant.shape
     hidden = mix_weight.shape[0]
@@ -160,6 +188,40 @@
     for stage in range(stages):
         greet(partner(stage))
 
+    loads = {
+        "courant": (courant_hbm, courant),
+        "adjoint_level": (adjoint_level_hbm, adj.at[1]),
+        "wave_level": (wave_level_hbm, wave.at[1]),
+        "receiver_cells": (receiver_cells_hbm, receiver_cells),
+        "residual": (residual_hbm, residual),
+        "source_cells": (source_cells_hbm, source_cells),
+        "wavelet": (wavelet_hbm, wavelet),
+        "step": (step_hbm, step_ref),
+        "wave_above": (wave_above_hbm, wave.at[0]),
+        "adjoint_above": (adjoint_above_hbm, adj.at[0]),
+        "cotangent": (cotangent_hbm, cotangent),
+        "rep_ref": (rep_ref_hbm, rep_ref),
+        "conv_weight": (conv_weight_hbm, conv_weight),
+        "sel_ref": (sel_ref_hbm, sel_ref),
+        "block_ref": (block_ref_hbm, block_ref),
+        "mix_weight": (mix_weight_hbm, mix_weight),
+        "back_ref": (back_ref_hbm, back_ref),
+        "conv_bias": (conv_bias_hbm, conv_bias),
+        "mix_bias": (mix_bias_hbm, mix_bias),
+        "out_weight": (out_weight_hbm, out_weight),
+        "place_ref": (place_ref_hbm, place_ref),
+    }
+    loads = {
+        name: pltpu.make_async_copy(src, dst, in_sem.at[index])
+        for index, (name, (src, dst)) in enumerate(loads.items())
+    }
+    for copy in loads.values():
+        copy.start()
+
+    def loaded(*wanted):
+        for name in wanted:
+            loads.pop(name).wait()
+
     def remote(src, dst, ssem, rsem, target):
         return pltpu.make_async_remote_copy(
             src_ref=src,
@@ -233,11 +295,8 @@
         spread_halo.at[1],
     )
 
-    wave[0] = wave_above[...]
-    wave[1] = wave_level[...]
-    adj[0] = adjoint_above[...]
-    adj[1] = adjoint_level[...]
-    scaled[0] = courant[...] * adjoint_level[...]
+    loaded("courant", "adjoint_level", "wave_level")
+    scaled[0] = courant[...] * adj[1]
     bf_planes[1] = courant[...].astype(BF16)
 
     def clear(side):
@@ -273,6 +332,7 @@
         hit = lax.broadcasted_iota(jnp.int32, (ny, count), 0) == cells[2:3, :]
         return jnp.where(hit, 1.0, 0.0).astype(BF16)
 
+    loaded("receiver_cells", "residual", "source_cells", "wavelet", "step")
     onehot_rec[...] = column_hot(receiver_cells)
     source_rows = jnp.where(row_hot(source_cells), 1.0, 0.0).astype(BF16)
     source_count = dot_nt(source_rows, column_hot(source_cells))
@@ -315,6 +375,12 @@
         return dot_nt(top, columns) + (dot_nt(middle, columns) + dot_nt(low, columns))
 
     image_out[...] = jnp.zeros(image_out.shape, F32)
+    stores = []
+
+    def store(index, src, dst):
+        copy = pltpu.make_async_copy(src, dst, out_sem.at[index])
+        copy.start()
+        stores.append(copy)
 
     def turn_of(turn):
         level = NSTEP - turn
@@ -362,12 +428,13 @@
             window[z, half, pl.ds(SR + 18, nx, stride=SR), :] = jnp.ones((nx, 128), F32)
     for p in range(planes):
         put_plane(1, p + 1, bf_planes[1, p].astype(F32))
+    loaded(*tuple(loads))
     cot_rows[...] = cotangent[...].astype(F32)
 
     wide = (RB + 2) * SR
     tall = RB * hidden
     rep = rep_ref[...]
-    tiled = dot_nt(rep, conv_weight[...]).astype(BF16)
+    tiled = dot(rep, conv_weight[...]).astype(BF16)
     row_block = lax.broadcasted_iota(jnp.int32, (tall, wide), 0) // hidden
     band = [row_block + b == block_ref[...] for b in range(3)]
     conv_banded = jnp.zeros((tall, wide), F32)
@@ -387,7 +454,7 @@
     back_column = lax.broadcasted_iota(jnp.int32, (back_rows, tall), 1) // hidden
     taps_banded = jnp.zeros((back_rows, tall), F32)
     for b in range(3):
-        part = dot_nt(dot(back_ref[b], conv_weight[...]).astype(BF16), rep)
+        part = dot_nt(dot_nt(back_ref[b], conv_weight[...]).astype(BF16), rep)
         taps_banded += jnp.where(back_column + b == back_row, part, 0.0)
     t_taps[...] = taps_banded.astype(BF16)
     rep_wide = rep.astype(F32)
@@ -413,7 +480,9 @@
     for p in range(planes):
         bf_planes[0, p] = image_out[p].astype(BF16)
     bf_pair(0)[0]()
-    second_out[...] = adj[NSTEP]
+    store(0, image_out, image_out_hbm)
+    store(1, first_out, first_out_hbm)
+    store(2, adj.at[NSTEP], second_out_hbm)
     for p in range(planes):
         put_plane(0, p + 1, bf_planes[0, p].astype(F32))
     bf_pair(1)[1]()
@@ -527,6 +596,7 @@
     spread_pair[1]()
     input_out[0] += spread_halo[0]
     input_out[planes - 1] += spread_halo[1]
+    store(3, input_out, input_out_hbm)
 
     summed = reduce_send[stages] * grad_scale
     eye = (
@@ -540,12 +610,17 @@
         preferred_element_type=F32,
         precision=lax.Precision.HIGHEST,
     )
-    taps = conv_weight.shape[0]
-    grad_conv_out[...] = turned[0:taps]
+    grad_conv_out[...] = summed[:, 0 : conv_weight.shape[1]]
     grad_conv_bias_out[...] = turned[LANE_BIAS : LANE_BIAS + 1]
     grad_mix_out[...] = turned[LANE_MIX : LANE_MIX + hidden]
     grad_mix_bias_out[...] = turned[LANE_MIX_BIAS : LANE_MIX_BIAS + 1]
     grad_out_out[...] = turned[LANE_OUT : LANE_OUT + 1]
+
+    store(4, grad_conv_out, grad_conv_out_hbm)
+    store(5, grad_conv_bias_out, grad_conv_bias_out_hbm)
+    store(6, grad_mix_out, grad_mix_out_hbm)
+    store(7, grad_mix_bias_out, grad_mix_bias_out_hbm)
+    store(8, grad_out_out, grad_out_out_hbm)
 
     for turn in range(NSTEP):
         for field in range(2):
@@ -555,6 +630,21 @@
     spread_pair[2]()
     for stage in range(stages):
         reduce_copy(stage).wait_send()
+    for copy in stores:
+        copy.wait()
+
+
+def hand_over(*refs):
+    count = len(refs) // 2
+    sem = refs[-1]
+    copies = [
+        pltpu.make_async_copy(refs[index], refs[count + index], sem.at[index])
+        for index in range(count)
+    ]
+    for copy in copies:
+        copy.start()
+    for copy in copies:
+        copy.wait()
 
 
 def on_device(
@@ -584,24 +674,44 @@
     grid = (planes, nx, ny)
     tall = RB * hidden
     wide = (RB + 2) * SR
-    vmem = pl.BlockSpec(memory_space=pltpu.VMEM)
-    smem = pl.BlockSpec(memory_space=pltpu.SMEM)
+    hbm = pl.BlockSpec(memory_space=pltpu.HBM)
     consts = constants(taps, hidden)
+    operands = (
+        checkpoint_step,
+        courant,
+        wave_level,
+        wave_above,
+        adjoint_level,
+        adjoint_above,
+        residual_data,
+        wavelet[None],
+        source_cells,
+        receiver_cells,
+        conv_weight.T,
+        conv_bias[None],
+        mix_weight,
+        mix_bias[None],
+        out_weight[None],
+        update_cotangent,
+        *consts,
+    )
+    kept = operands[1:2] + operands[6:]
+    out_shape = (
+        jax.ShapeDtypeStruct(grid, F32),
+        jax.ShapeDtypeStruct(grid, F32),
+        jax.ShapeDtypeStruct(grid, F32),
+        jax.ShapeDtypeStruct(grid, F32),
+        jax.ShapeDtypeStruct((hidden, taps), F32),
+        jax.ShapeDtypeStruct((1, hidden), F32),
+        jax.ShapeDtypeStruct((hidden, hidden), F32),
+        jax.ShapeDtypeStruct((1, hidden), F32),
+        jax.ShapeDtypeStruct((1, hidden), F32),
+    )
     outs = pl.pallas_call(
         functools.partial(kernel, n, grad_scale),
-        out_shape=(
-            jax.ShapeDtypeStruct(grid, F32),
-            jax.ShapeDtypeStruct(grid, F32),
-            jax.ShapeDtypeStruct(grid, F32),
-            jax.ShapeDtypeStruct(grid, F32),
-            jax.ShapeDtypeStruct((taps, hidden), F32),
-            jax.ShapeDtypeStruct((1, hidden), F32),
-            jax.ShapeDtypeStruct((hidden, hidden), F32),
-            jax.ShapeDtypeStruct((1, hidden), F32),
-            jax.ShapeDtypeStruct((1, hidden), F32),
-        ),
-        in_specs=[smem] + [vmem] * (15 + len(consts)),
-        out_specs=(vmem,) * 9,
+        out_shape=out_shape,
+        in_specs=[hbm] * len(operands),
+        out_specs=(hbm,) * 9,
         scratch_shapes=[
             pltpu.VMEM((NSTEP + 1,) + grid, F32),
             pltpu.VMEM((NSTEP + 1,) + grid, F32),
@@ -629,30 +739,27 @@
             pltpu.SemaphoreType.DMA((EXCH_COUNT, 2)),
             pltpu.SemaphoreType.DMA((max(stages, 1),)),
             pltpu.SemaphoreType.DMA((max(stages, 1),)),
-        ],
+            pltpu.SemaphoreType.DMA((len(operands),)),
+            pltpu.SemaphoreType.DMA((9,)),
+        ]
+        + [pltpu.VMEM(out_shape[index].shape, F32) for index in range(9) if index != 2]
+        + [
+            pltpu.SMEM((1,), jnp.int32),
+        ]
+        + [pltpu.VMEM(array.shape, array.dtype) for array in kept],
         compiler_params=pltpu.CompilerParams(
-            collective_id=0, has_side_effects=True, vmem_limit_bytes=48 * 1024 * 1024
+            collective_id=0, has_side_effects=True, vmem_limit_bytes=VMEM_LIMIT
         ),
-    )(
-        checkpoint_step,
-        courant,
-        wave_level,
-        wave_above,
-        adjoint_level,
-        adjoint_above,
-        residual_data,
-        wavelet[None],
-        source_cells,
-        receiver_cells,
-        conv_weight,
-        conv_bias[None],
-        mix_weight,
-        mix_bias[None],
-        out_weight[None],
-        update_cotangent,
-        *consts,
-    )
-    return outs[:5] + (outs[5][0], outs[6], outs[7][0], outs[8][0])
+    )(*operands)
+    outs = pl.pallas_call(
+        hand_over,
+        out_shape=tuple(jax.ShapeDtypeStruct(array.shape, array.dtype) for array in outs),
+        in_specs=[hbm] * len(outs),
+        out_specs=(hbm,) * len(outs),
+        scratch_shapes=[pltpu.SemaphoreType.DMA((len(outs),))],
+        compiler_params=pltpu.CompilerParams(vmem_limit_bytes=VMEM_LIMIT),
+    )(*outs)
+    return outs[:4] + (outs[4].T, outs[5][0], outs[6], outs[7][0], outs[8][0])
 
 
 def solution(mesh):

time: 80.4 us -> 82.2 us (1.022)
  Pallas kernels: 61.5 us -> 80.4 us
  local copies, waits for them, and re-layouts: 16.7 us -> 0 us
    pallas_call x1 -> x2, Pallas kernels: 61.5 us -> 80.4 us  [the longest x1 62.3 us: on_device(): pl.pallas_call(functools.partial(kernel, n, grad_scale), out_shape=out_sh...]
    unnamed x48 -> x0, local copies, waits for them, and re-layouts: 16.7 us -> none
where the time goes in v2:
time: 82.2 us; the launch traced here: 81.7 us
  Pallas kernels  80.4 us (98%)
  between operations  1.3 us (2%)
    pallas_call x1, Pallas kernels, on_device(): pl.pallas_call(functools.partial(kernel, n, grad_scale), out_shape=out_sh...  62.3 us
    pallas_call x1, Pallas kernels, on_device(): pl.pallas_call(hand_over, out_shape=tuple((jax.ShapeDtypeStruct(array.sha...  18.1 us

profile of v2, /device:TPU:0, one launch (start us, length us, event | category | flops | bytes accessed | tf_op | source)
XLA Modules:
  0.0 81.7 jit_solution(15996008304491083668)
XLA Ops:
  1.3 62.3 %shard_map.268 = (f32[2,64,256]{2,1,0:T(8,128)}, f32[2,64,256]{2,1,0:T(8,128)}, f32[2,64,256]{2,1,0:T(8,128)}, f32[2,64,256]{2,1,0:T(8,128)}, f32[32,54]{1,0:T(8...) custom-call(s32[1]{0:T(128)S(6)} %copy.30.step_hbm, ...), custom_call_target="tpu_custom_call" | custom-call | tf_op jit(solution)/shard_map/pallas_call | solution.py:710
  63.6 18.1 %shard_map.269 = (f32[2,64,256]{2,1,0:T(8,128)}, f32[2,64,256]{2,1,0:T(8,128)}, f32[2,64,256]{2,1,0:T(8,128)}, f32[2,64,256]{2,1,0:T(8,128)}, f32[32,54]{1,0:T(8...) custom-call(f32[2,64,256]{2,1,0:T(8,128)} %get-tuple-element.27.refs_0_, ...), custom_call_target="tpu_custom_call" | custom-call | tf_op jit(solution)/shard_map/pallas_call | solution.py:754
